TPU v7x, 768 devices: a whole 4x8x12 slice. The times are simulated.
768 devices in a mesh: task: 96 (over z, y), blk: 8 (over x, core).
Axes of the slice: x: 4, y: 8, z: 12, core: 2. Of those that a mesh axis runs over, the one named last changes fastest.
Arguments:
- coeffs: bfloat16 [6144, 96, 1024], P(('task', 'blk')), may hold values from -1.09375 to 1.09375
- coulomb: bfloat16 [3072, 9216], P(('task', 'blk')), may hold values from -0.625 to 0.625
- density: bfloat16 [512, 1024], P('blk'), may hold values from -6 to 6
- task_owner: int32 [49152, 1], P(('task', 'blk')), may hold values from 0 to 7; in each aligned block of 64 rows (0 to 63, 64 to 127, ...) at most 16 rows name the same one
- task_slot: int32 [49152], P(('task', 'blk')), may hold values from 0 to 63
- task_left: int32 [49152], P(('task', 'blk')), may hold values from 0 to 7
- task_right: int32 [49152], P(('task', 'blk')), may hold values from 0 to 7
- task_aux: int32 [49152], P(('task', 'blk')), may hold values from 0 to 3
- task_dest: int32 [49152], P(('task', 'blk')), may hold values from 0 to 767, as said below
Outputs:
- exchange_k: float32 [768, 1024], P(('task', 'blk'))
Inputs may be any that keep to these rules, and one draw needn't show every extreme that they name: `task_owner`: among the tasks of one device no owner is named by more than 16 tasks, and some device reaches 16. Among the tasks of one device at most 16 have a task_dest with the same remainder modulo 8, and every device reaches 16 for some remainder.
All inputs are finite; a program needn't handle non-finite values.
Results may differ from a plain program's by a relative error of at most 0.0041.
Values may be sent and summed in bfloat16 or wider, within the bound.
No kernel may reach another device: no remote copies, remote signals or barrier semaphores. Data moves between devices by JAX's collectives and lax.ppermute only.
A program may use at most 32 MiB of HBM per device.

v0:
```python
import jax
import jax.numpy as jnp
from jax import lax
from jax.sharding import PartitionSpec as P

KDEV = 1


def group_work(coeffs, coulomb, pieces):
    left_rows, right_rows, aux_rows, fetched_rows = pieces
    group_size = left_rows.shape[0]
    na_count = coeffs.shape[1]
    no_count = fetched_rows.shape[1]
    no_side = int(round(no_count**0.5))
    left_blocks = coeffs[left_rows].reshape(group_size, na_count, no_side, no_side)
    right_blocks = coeffs[right_rows].reshape(group_size, na_count, no_side, no_side)
    coulomb_blocks = coulomb[aux_rows].reshape(group_size, na_count, na_count)
    density_blocks = fetched_rows.reshape(group_size, no_side, no_side)
    contracted = jnp.einsum(
        "tnjl,tkl->tnjk", right_blocks, density_blocks, preferred_element_type=jnp.float32
    ).astype(jnp.bfloat16)
    applied = jnp.einsum(
        "tmn,tnjk->tmjk", coulomb_blocks, contracted, preferred_element_type=jnp.float32
    ).astype(jnp.bfloat16)
    partial_k = jnp.einsum(
        "tmik,tmjk->tij", left_blocks, applied, preferred_element_type=jnp.float32
    )
    return partial_k.reshape(group_size, no_count)


def per_device(
    coeffs, coulomb, density, task_owner, task_slot, task_left, task_right, task_aux, task_dest
):
    task_count = task_slot.shape[0]
    block_cells = density.shape[1]
    blk_count = lax.axis_size("blk")
    task_count_axis = lax.axis_size("task")
    owner_rows = task_owner[:, 0]
    local_blocks = density.shape[0]
    wanted = owner_rows * local_blocks + task_slot
    shard_rows = lax.all_gather(density, "blk", axis=0, tiled=True)
    inside_range = (wanted >= 0) & (wanted < shard_rows.shape[0])
    chosen = shard_rows[jnp.clip(wanted, 0, shard_rows.shape[0] - 1)]
    fetched = jnp.where(
        inside_range[:, None], chosen, jnp.zeros((task_count, block_cells), jnp.bfloat16)
    )
    group_size = 8
    groups = task_count // group_size
    stacked = (
        task_left.reshape(groups, group_size),
        task_right.reshape(groups, group_size),
        task_aux.reshape(groups, group_size),
        fetched.reshape(groups, group_size, block_cells),
    )
    partials = lax.map(lambda pieces: group_work(coeffs, coulomb, pieces), stacked)
    partials = partials.reshape(task_count, block_cells)
    k_rows = KDEV * task_count_axis * blk_count
    k_dense = jnp.zeros((k_rows, block_cells), jnp.float32).at[task_dest].add(partials)
    summed = lax.psum_scatter(k_dense, ("task", "blk"), scatter_dimension=0, tiled=True)
    return -0.25 * summed


def solution(mesh):
    placed = (
        P(("task", "blk"), None, None),
        P(("task", "blk"), None),
        P("blk", None),
        P(("task", "blk"), None),
        P(("task", "blk")),
        P(("task", "blk")),
        P(("task", "blk")),
        P(("task", "blk")),
        P(("task", "blk")),
    )
    return jax.shard_map(
        per_device, mesh=mesh, in_specs=placed, out_specs=P(("task", "blk"), None), check_vma=False
    )
```

profile of v0, /device:TPU:1, one launch (start us, length us, event | category | flops | bytes accessed | tf_op | source)
XLA Modules:
  0.0 690.1 jit_solution(10815734926167306442)
XLA Ops:
  11.6 37.8 %all-gather.2.cloned.1.call-done = bf16[512,1024]{1,0:T(8,128)(2,1)} async-done(((bf16[64,1024]{1,0:T(8,128)(2,1)}), bf16[512,1024]{1,0:T(8,128)(2,1)}) %all-gather.2.cloned.1.call-update) | async-done | bytes 1048592 | tf_op jit(solution)/shard_map/all_gather | solution.py:41
  51.6 143.5 %while.10 = (s32[]{:T(128)}, f32[8,8,1024]{2,1,0:T(8,128)S(1)}, s32[8,8]{1,0:T(8,128)S(1)}, bf16[8,96,1024]{2,1,0:T(8,128)(2,1)}, s32[8,8]{1,0:T(8,128)S(1)}, /*...) while((s32[]{:T(128)}, f32[8,8,1024]{2,1,0:T(8,128)S(1)}, ...), condition=%wide.region_1.2_spmd, body=%wide.region_0.1_spmd.sunk | while | flops 253234240 | bytes 20165128 | solution.py:55
  51.7 3.2 gather_fusion
  54.9 2.9 copy.41
  62.1 2.4 copy.42
  65.3 4.1 fusion.46
  69.6 3.2 gather_fusion
  72.8 2.9 copy.41
  80.0 2.4 copy.42
  83.3 4.1 fusion.46
  87.6 3.2 gather_fusion
  90.8 2.9 copy.41
  98.0 2.4 copy.42
  101.2 4.1 fusion.46
  105.5 3.2 gather_fusion
  108.7 2.9 copy.41
  115.9 2.4 copy.42
  119.1 4.1 fusion.46
  123.4 3.2 gather_fusion
  126.7 2.9 copy.41
  137.1 4.1 fusion.46
  141.4 3.2 gather_fusion
  144.6 2.9 copy.41
  155.0 4.1 fusion.46
  159.3 3.2 gather_fusion
  162.5 2.9 copy.41
  172.9 4.1 fusion.46
  177.2 3.2 gather_fusion
  180.5 2.9 copy.41
  190.9 4.1 fusion.46
  195.1 2.9 scatter_custom_fusion
  198.1 483.8 %all-reduce.3.cloned.1.call-done = f32[768,1024]{1,0:T(8,128)} async-done(((f32[768,1024]{1,0:T(8,128)}), f32[768,1024]{1,0:T(8,128)}) %all-reduce.3.cloned.1.call-update) | async-done | bytes 3145744
  (140 shorter events, 59.7 us)
Async XLA Ops:
  6.5 42.9 %all-gather.2.cloned.1.call-start = ((), (), s32[]{:S(2)}) async-start(), calls=%async_computation | async-start | bytes 1179648 | tf_op jit(solution)/shard_map/all_gather | solution.py:41
  7.3 674.7 %all-reduce.3.cloned.1.call-start = ((), (), s32[]{:S(2)}) async-start(), calls=%async_computation.1 | async-start | bytes 6291456
  62.1 2.4 copy-start
  80.0 2.4 copy-start
  97.9 2.4 copy-start
  115.9 2.4 copy-start
  133.8 2.4 copy-start
  151.7 2.4 copy-start
  169.7 2.4 copy-start
  187.6 2.4 copy-start
Sparse Core Ops, SparseCore 0:
  9.8 39.5 all-gather.1
  198.2 483.6 all-reduce.2
where the time goes:
time: 691 us; the launch traced here: 690 us
  waiting for transfers between devices  522 us (76%)
  local copies, waits for them, and re-layouts  97.8 us (14%)
  matrix products  49.1 us (7%)
  between operations  13.4 us (2%)
    unnamed x3, waiting for transfers between devices  485 us
    gather x16, local copies, waits for them, and re-layouts, group_work(): coeffs[right_rows].reshape(group_size, na_count, no_side, no_side)  49.2 us
    all_gather x1, waiting for transfers between devices, per_device(): shard_rows = lax.all_gather(density, 'blk', axis=0, tiled=True)  37.8 us
    gather x16, local copies, waits for them, and re-layouts, group_work(): coeffs[left_rows].reshape(group_size, na_count, no_side, no_side)  35.7 us
    dot_general x8, matrix products, group_work(): jnp.einsum('tmik,tmjk->tij', left_blocks, applied, preferred_element_type...  32.9 us
    dot_general x8, matrix products, group_work(): jnp.einsum('tnjl,tkl->tnjk', right_blocks, density_blocks, preferred_elem...  16.1 us
  transfers between devices with their start and end apart: 2, of which 2 were waited for; matrix products, arithmetic and copies ran while one was open for 1% of the time, Pallas kernels for 0%

commit v1 on v0

v1 whole, which is shorter than its diff:
```python
import functools
import jax
import jax.numpy as jnp
from jax import lax
from jax.experimental import pallas as pl
from jax.experimental.pallas import tpu as pltpu

BF = jnp.bfloat16
F32 = jnp.float32
VM = pl.BlockSpec(memory_space=pltpu.VMEM)
SM = pl.BlockSpec(memory_space=pltpu.SMEM)


def chunk_of():
    return lax.broadcasted_iota(jnp.int32, (8, 128), 1) // 32


def turn(y_ref, base):
    chunk = chunk_of()
    even = chunk % 2 == 0
    low = chunk < 2
    halves = []
    for h in range(2):
        x = [y_ref[pl.ds(base + 4 * h + m, 8, stride=8), :] for m in range(4)]
        y = [None] * 4
        for p in (0, 2):
            y[p] = jnp.where(even, x[p], pltpu.roll(x[p + 1], 32, 1))
            y[p + 1] = jnp.where(even, pltpu.roll(x[p], 96, 1), x[p + 1])
        z = [None] * 4
        for p in (0, 1):
            moved = pltpu.roll(jnp.where(low, y[p + 2], y[p]), 64, 1)
            z[p] = jnp.where(low, y[p], moved)
            z[p + 2] = jnp.where(low, moved, y[p + 2])
        halves.append(jnp.concatenate(z, axis=0))
    return jnp.concatenate(halves, axis=1).astype(BF)


def prepare(coeffs_ref, coulomb_ref, w_ref, l_ref, y_ref):
    blocks, na, cells = coeffs_ref.shape
    vrows = coulomb_ref.shape[0]
    aux = vrows // na
    tiles = na // 8

    def one(r, carry):
        vall = coulomb_ref[...]
        for q in range(cells // 256):
            right = coeffs_ref[r, :, q * 256:(q + 1) * 256]
            y = jnp.dot(vall, right, preferred_element_type=F32)
            full = jnp.concatenate([y, right.astype(F32)], axis=0)
            for e in range(2):
                v = 2 * q + e
                for mt in range((vrows + na) // 8):
                    y_ref[mt * 64 + v * 8:mt * 64 + v * 8 + 8, :] = full[mt * 8:mt * 8 + 8, e * 128:(e + 1) * 128]

        def one_tile(s, c):
            for a in range(aux):
                w_ref[r * aux + a, pl.ds(pl.multiple_of(s * 32, 32), 32), :] = turn(y_ref, (a * tiles + s) * 64)
            l_ref[s, pl.ds(pl.multiple_of(r * 32, 32), 32), :] = turn(y_ref, (aux * tiles + s) * 64)
            return c

        lax.fori_loop(0, tiles, one_tile, 0)
        return carry

    lax.fori_loop(0, blocks, one, 0)


def run_prepare(coeffs, vall):
    blocks, na, cells = coeffs.shape
    aux = vall.shape[0] // na
    tiles = na // 8
    return pl.pallas_call(
        prepare,
        out_shape=(
            jax.ShapeDtypeStruct((blocks * aux, tiles * 32, 256), BF),
            jax.ShapeDtypeStruct((tiles, blocks * 32, 256), BF),
        ),
        in_specs=[VM, VM],
        out_specs=(VM, VM),
        scratch_shapes=[pltpu.VMEM(((vall.shape[0] + na) * 8, 128), F32)],
        compiler_params=pltpu.CompilerParams(vmem_limit_bytes=48 * 2**20),
    )(coeffs, vall)


def tasks_kernel(me_ref, owner_ref, slot_ref, left_ref, right_ref, aux_ref, dest_ref, w_ref, l_ref, d_ref,
                 out_ref, a_ref, p_ref, count_ref):
    tasks = slot_ref.shape[0]
    peers, cap = out_ref.shape[0], out_ref.shape[1] - 1
    tiles = l_ref.shape[0]
    aux = w_ref.shape[0] // 8
    out_ref[...] = jnp.zeros_like(out_ref)
    for b in range(peers):
        count_ref[b] = 0

    row = lax.broadcasted_iota(jnp.int32, (256, 64), 0)
    col = lax.broadcasted_iota(jnp.int32, (256, 64), 1)
    spread = (row // 4 == col).astype(F32).astype(BF)
    krow = lax.broadcasted_iota(jnp.int32, (256, 128), 0)
    kchunk = lax.broadcasted_iota(jnp.int32, (256, 128), 1) // 32
    own_chunk = krow % 4 == kchunk
    pr = lax.broadcasted_iota(jnp.int32, (128, 256), 0)
    pc = lax.broadcasted_iota(jnp.int32, (128, 256), 1)
    repeat = (pr % 32 == pc % 32).astype(F32).astype(BF)
    br = lax.broadcasted_iota(jnp.int32, (256, 256), 0)
    bc = lax.broadcasted_iota(jnp.int32, (256, 256), 1)
    diag = (br // 32 == bc // 32).astype(F32).astype(BF)
    chunk = chunk_of()
    lane = lax.broadcasted_iota(jnp.int32, (8, 128), 1)
    me = me_ref[0]

    def group(g, carry):
        base = g * 8
        picked = [d_ref[owner_ref[base + t] * 64 + slot_ref[base + t]].astype(F32) for t in range(8)]
        stacked = jnp.concatenate(picked, axis=0).astype(BF)
        e = jnp.dot(spread, stacked, preferred_element_type=F32)
        e = jnp.where(own_chunk, e, 0.0).astype(BF)
        dl = jnp.dot(e, repeat, preferred_element_type=F32).astype(BF)
        for t in range(8):
            bd = jnp.concatenate([dl[t * 32:(t + 1) * 32]] * 8, axis=0) * diag
            w = w_ref[right_ref[base + t] * aux + aux_ref[base + t]]
            y = lax.dot_general(w, bd, (((1,), (1,)), ((), ())), preferred_element_type=F32).astype(BF)
            for s in range(tiles):
                a_ref[t * 32:(t + 1) * 32, s * 256:(s + 1) * 256] = y[s * 32:(s + 1) * 32, :]
        total = jnp.zeros((256, 256), F32)
        for s in range(tiles):
            total += lax.dot_general(l_ref[s], a_ref[:, s * 256:(s + 1) * 256], (((1,), (1,)), ((), ())), preferred_element_type=F32)
        p_ref[...] = total
        for t in range(8):
            top = left_ref[base + t] * 32
            half, mine = t // 4, t % 4
            block = None
            for q in range(4):
                piece = p_ref[pl.ds(pl.multiple_of(top + q * 8, 8), 8), half * 128:(half + 1) * 128]
                if q != mine:
                    piece = pltpu.roll(piece, ((q - mine) * 32) % 128, 1)
                block = piece if block is None else jnp.where(chunk == q, piece, block)
            dest = dest_ref[base + t]
            peer = lax.rem(dest, peers)
            place = count_ref[peer]
            count_ref[peer] = place + 1
            out_ref[peer, place] = block
            name = (dest // peers + 1).astype(F32)
            out_ref[peer, cap] = jnp.where(lane == me * cap + place, name, out_ref[peer, cap])
        return carry

    lax.fori_loop(0, tasks // 8, group, 0)


def run_tasks(me, owner, slot, left, right, aux, dest, w, l, dens, peers, cap):
    return pl.pallas_call(
        tasks_kernel,
        out_shape=jax.ShapeDtypeStruct((peers, cap + 1, 8, 128), F32),
        in_specs=[SM] * 7 + [VM] * 3,
        out_specs=VM,
        scratch_shapes=[
            pltpu.VMEM((256, l.shape[0] * 256), BF),
            pltpu.VMEM((256, 256), F32),
            pltpu.SMEM((peers,), jnp.int32),
        ],
        compiler_params=pltpu.CompilerParams(vmem_limit_bytes=48 * 2**20),
    )(me, owner, slot, left, right, aux, dest, w, l, dens)


def spread_kernel(recv_ref, out_ref, flat_ref):
    peers, slots = recv_ref.shape[0], recv_ref.shape[1]
    cap = slots - 1
    rows = out_ref.shape[0]
    names = recv_ref[0, cap]
    for p in range(1, peers):
        names = names + recv_ref[p, cap]
    wanted = lax.broadcasted_iota(jnp.int32, (rows, 128), 0) + 1
    hot = (wanted == jnp.broadcast_to(names[0:1, :], (rows, 128)).astype(jnp.int32)).astype(F32).astype(BF)
    for p in range(peers):
        for n in range(cap):
            flat_ref[(p * cap + n) * 8:(p * cap + n + 1) * 8, :] = recv_ref[p, n]
    sums = []
    for i in range(8):
        x = flat_ref[pl.ds(i, 128, stride=8), :]
        hi = x.astype(BF)
        lo = (x - hi.astype(F32)).astype(BF)
        both = jnp.dot(hot, hi, preferred_element_type=F32) + jnp.dot(hot, lo, preferred_element_type=F32)
        flat2 = both
        sums.append(flat2)
    for i in range(8):
        flat_ref[pl.ds(i, rows, stride=8), :] = sums[i]
    out_ref[...] = flat_ref[0:rows * 8, :].reshape(rows, 8, 128).astype(out_ref.dtype)


def run_spread(recv, rows, dtype):
    peers, slots = recv.shape[:2]
    return pl.pallas_call(
        spread_kernel,
        out_shape=jax.ShapeDtypeStruct((rows, 8, 128), dtype),
        in_specs=[VM],
        out_specs=VM,
        scratch_shapes=[pltpu.VMEM((max(rows, peers * (slots - 1)) * 8, 128), F32)],
        compiler_params=pltpu.CompilerParams(vmem_limit_bytes=32 * 2**20),
    )(recv)


def final_kernel(recv_ref, out_ref):
    rows = recv_ref.shape[0]
    total = jnp.sum(recv_ref[...].astype(F32), axis=0) * -0.25
    r = lax.broadcasted_iota(jnp.int32, (128, 128), 0)
    c = lax.broadcasted_iota(jnp.int32, (128, 128), 1)
    source = (c // 32) * 32 + (c % 4) * 8 + (c % 32) // 4
    move = (r == source).astype(F32)
    out_ref[...] = jnp.dot(total, move, preferred_element_type=F32, precision=lax.Precision.HIGHEST)


def run_final(recv):
    return pl.pallas_call(
        final_kernel,
        out_shape=jax.ShapeDtypeStruct((8, 128), F32),
        in_specs=[VM],
        out_specs=VM,
    )(recv)
def per_device(coeffs, coulomb, density, task_owner, task_slot, task_left, task_right, task_aux, task_dest):
    na = coeffs.shape[1]
    blk, task = lax.axis_size("blk"), lax.axis_size("task")
    w, l = run_prepare(coeffs, coulomb.reshape(coulomb.shape[0] * na, na))
    mine = density.reshape(density.shape[0], 8, 128)
    dens = lax.all_to_all(jnp.broadcast_to(mine, (blk, *mine.shape)), "blk", 0, 0, tiled=True)
    dens = dens.reshape(blk * mine.shape[0], 8, 128)
    me = lax.axis_index("blk").astype(jnp.int32).reshape(1)
    send = run_tasks(me, task_owner.reshape(-1), task_slot, task_left, task_right, task_aux, task_dest, w, l, dens, blk, 16)
    recv = lax.all_to_all(send, "blk", 0, 0, tiled=True)
    rows = run_spread(recv, task, BF)
    back = lax.all_to_all(rows, "task", 0, 0, tiled=True)
    return run_final(back).reshape(1, 1024)


def solution(mesh):
    from jax.sharding import PartitionSpec as P
    both = P(("task", "blk"))
    placed = (P(("task", "blk"), None, None), P(("task", "blk"), None), P("blk", None), P(("task", "blk"), None), both, both, both, both, both)
    return jax.shard_map(per_device, mesh=mesh, in_specs=placed, out_specs=P(("task", "blk"), None), check_vma=False)
```

time: 691 us -> 108 us (0.16)
  waiting for transfers between devices: 522 us -> 0.01 us
  local copies, waits for them, and re-layouts: 97.8 us -> 4.82 us
  matrix products: 49.1 us -> 0 us
  Pallas kernels: 0 us -> 44.1 us
  blocking collectives: 0 us -> 44 us
  starting transfers between devices: 0.04 us -> 14.1 us
  between operations: 13.4 us -> 0.12 us
    unnamed x3 -> x0, waiting for transfers between devices: 485 us -> none
    gather x41 -> x0, local copies, waits for them, and re-layouts: 92 us -> none  [the longest x16 49.2 us: group_work(): coeffs[right_rows].reshape(group_size, na_count, no_side, no_side)]
    dot_general x16 -> x0, matrix products: 49.1 us -> none  [the longest x8 32.9 us: group_work(): jnp.einsum('tmik,tmjk->tij', left_blocks, applied, preferred_element_type...]
    pallas_call x0 -> x4, Pallas kernels: none -> 44.1 us  [the longest x1 21.2 us: run_prepare(): pl.pallas_call(prepare, out_shape=(jax.ShapeDtypeStruct((blocks * aux, ti...]
    all_to_all x0 -> x2, blocking collectives: none -> 44 us  [the longest x1 29.2 us: per_device(): back = lax.all_to_all(rows, 'task', 0, 0, tiled=True)]
    all_gather x1 -> x0, waiting for transfers between devices: 37.8 us -> none  [per_device(): shard_rows = lax.all_gather(density, 'blk', axis=0, tiled=True)]
    all_to_all x0 -> x1, starting transfers between devices: none -> 14.1 us  [per_device(): lax.all_to_all(jnp.broadcast_to(mine, (blk, *mine.shape)), 'blk', 0, 0, t...]
  transfers between devices with their start and end apart: 2 -> 1, of which waited for: 2 -> 0; matrix products, arithmetic and copies ran while one was open for 1% -> 0% of each run, Pallas kernels for 0% -> 20%
where the time goes in v1:
time: 108 us; the launch traced here: 107 us
  Pallas kernels  44.1 us (41%)
  blocking collectives  44 us (41%)
  starting transfers between devices  14.1 us (13%)
  local copies, waits for them, and re-layouts  4.82 us (4%)
    all_to_all x1, blocking collectives, per_device(): back = lax.all_to_all(rows, 'task', 0, 0, tiled=True)  29.2 us
    pallas_call x1, Pallas kernels, run_prepare(): pl.pallas_call(prepare, out_shape=(jax.ShapeDtypeStruct((blocks * aux, ti...  21.2 us
    pallas_call x1, Pallas kernels, run_tasks(): pl.pallas_call(tasks_kernel, out_shape=jax.ShapeDtypeStruct((peers, cap +...  20.7 us
    all_to_all x1, blocking collectives, per_device(): recv = lax.all_to_all(send, 'blk', 0, 0, tiled=True)  14.8 us
    all_to_all x1, starting transfers between devices, per_device(): lax.all_to_all(jnp.broadcast_to(mine, (blk, *mine.shape)), 'blk', 0, 0, t...  14.1 us
    unnamed x21, local copies, waits for them, and re-layouts  3.51 us
  transfers between devices with their start and end apart: 1, of which 0 were waited for; matrix products, arithmetic and copies ran while one was open for 0% of the time, Pallas kernels for 20%

profile of v1, /device:TPU:1, one launch (start us, length us, event | category | flops | bytes accessed | tf_op | source)
XLA Modules:
  0.0 107.2 jit_solution(12596552299417509117)
XLA Ops:
  0.0 0.9 copy.10
  0.9 0.0 copy-start.9
  0.9 0.0 copy-start
  1.0 1.2 %broadcast_in_dim.3 = bf16[8,64,8,128]{3,2,1,0:T(8,128)(2,1)} broadcast(bf16[64,8,128]{2,1,0:T(8,128)(2,1)S(1)} %bitcast.8), dimensions={1,2,3} | broadcast | bytes 1179648 | tf_op jit(solution)/shard_map/broadcast_in_dim | solution.py:222
  2.1 0.0 copy-start.3
  2.1 0.0 copy-start.4
  2.1 0.0 copy-start.5
  2.1 0.0 copy-start.6
  2.2 0.0 copy-start.7
  2.2 0.0 copy-start.8
  2.2 14.1 %all-to-all-start = ((bf16[8,64,8,128]{3,2,1,0:T(8,128)(2,1)}), bf16[8,64,8,128]{3,2,1,0:T(8,128)(2,1)S(1)}, u32[]{:S(2)}, u32[]{:S(2)}) async-start(bf16[8,64,8,128]{3,2,1,0:T(8,128)(2,1)} %broadcast_in_dim.3), calls=%async_computation | async-start | bytes 2097152 | tf_op jit(solution)/shard_map/all_to_all | solution.py:222
  16.3 0.0 copy-done.9
  16.3 0.1 reshape.20.coulomb_ref
  16.4 0.0 copy-done
  16.4 21.2 %shard_map.91 = (bf16[32,384,256]{2,1,0:T(8,128)(2,1)}, bf16[12,256,256]{2,1,0:T(8,128)(2,1)S(1)}) custom-call(bf16[8,96,1024]{2,1,0:T(8,128)(2,1)S(1)} %copy-done, bf16[384,96]{1,0:T(8,128)(2,1)S(1)} %reshape.20.coulomb_ref), custom_call_target="tpu_custom_call" | custom-call | tf_op jit(solution)/shard_map/pallas_call | solution.py:71
  37.7 0.0 copy-start.1
  37.7 1.1 %copy-done.1 = bf16[12,256,256]{2,1,0:T(8,128)(2,1)} copy-done((bf16[12,256,256]{2,1,0:T(8,128)(2,1)}, bf16[12,256,256]{2,1,0:T(8,128)(2,1)S(1)}, u32[]{:S(2)}) %copy-start.1) | copy-done | bytes 1572888
  38.8 0.0 all-to-all-done
  38.8 0.0 copy-done.3
  38.8 0.0 copy-done.4
  38.8 0.0 copy-done.5
  38.9 0.0 copy-done.6
  38.9 0.0 copy-done.7
  38.9 0.0 copy-done.8
  38.9 0.0 copy-start.2
  38.9 1.4 %copy-done.2 = bf16[12,256,256]{2,1,0:T(8,128)(2,1)S(1)} copy-done((bf16[12,256,256]{2,1,0:T(8,128)(2,1)S(1)}, bf16[12,256,256]{2,1,0:T(8,128)(2,1)}, u32[]{:S(2)}) %copy-start.2) | copy-done | bytes 1572888
  40.3 20.7 %shard_map.92 = f32[8,17,8,128]{3,2,1,0:T(8,128)S(1)} custom-call(s32[1]{0:T(128)} %bitcast.me_ref, s32[64]{0:T(128)S(1)} %bitcast.7, s32[64]{0:T(128)S(1)} %copy-done.4, s32[64]{0:T(128)S(1)} %copy-done.5, s32[64]{0:T(128)S(1)} %copy-done.6, s32[64]{0:T(128)S(1)} %copy-done.7, s32[64]{0:T(128)S(1)} %copy-done.8, ...), custom_call_target="tpu_custom_call" | custom-call | tf_op jit(solution)/shard_map/pallas_call | solution.py:149
  61.0 14.8 %all_to_all.15.recv_ref = f32[8,17,8,128]{3,2,1,0:T(8,128)S(1)} all-to-all(f32[8,17,8,128]{3,2,1,0:T(8,128)S(1)} %shard_map.92), channel_id=1, replica_groups=mesh['task'=96,'blk'=8] {'blk'}, dimensions={0} | all-to-all | bytes 1114112 | tf_op jit(solution)/shard_map/all_to_all | solution.py:226
  75.8 0.4 shard_map.93
  76.2 29.2 %all_to_all.16.recv_ref = bf16[96,8,128]{2,1,0:T(8,128)(2,1)} all-to-all(bf16[96,8,128]{2,1,0:T(8,128)(2,1)S(1)} %shard_map.93), channel_id=1, replica_groups=mesh['task'=96,'blk'=8] {'task'}, dimensions={0} | all-to-all | bytes 393216 | tf_op jit(solution)/shard_map/all_to_all | solution.py:228
  105.4 1.8 %shard_map.94 = f32[8,128]{1,0:T(8,128)} custom-call(bf16[96,8,128]{2,1,0:T(8,128)(2,1)} %all_to_all.16.recv_ref), custom_call_target="tpu_custom_call" | custom-call | tf_op jit(solution)/shard_map/pallas_call | solution.py:211
Async XLA Ops:
  0.9 15.4 %copy-start.9 = (bf16[4,9216]{1,0:T(4,128)(2,1)S(1)}, bf16[4,9216]{1,0:T(4,128)(2,1)}, u32[]{:S(2)}) copy-start(bf16[4,9216]{1,0:T(4,128)(2,1)} %param.10) | copy-start | bytes 221188
  0.9 15.5 %copy-start = (bf16[8,96,1024]{2,1,0:T(8,128)(2,1)S(1)}, bf16[8,96,1024]{2,1,0:T(8,128)(2,1)}, u32[]{:S(2)}) copy-start(bf16[8,96,1024]{2,1,0:T(8,128)(2,1)} %coeffs_ref.1) | copy-start | bytes 4718596
  2.1 36.7 %copy-start.3 = (s32[64,1]{0,1:T(1,128)S(1)}, s32[64,1]{0,1:T(1,128)}, u32[]{:S(2)}) copy-start(s32[64,1]{0,1:T(1,128)} %param.12) | copy-start | bytes 772
  2.1 36.7 %copy-start.4 = (s32[64]{0:T(128)S(1)}, s32[64]{0:T(128)}, u32[]{:S(2)}) copy-start(s32[64]{0:T(128)} %slot_ref.1) | copy-start | bytes 772
  2.1 36.7 %copy-start.5 = (s32[64]{0:T(128)S(1)}, s32[64]{0:T(128)}, u32[]{:S(2)}) copy-start(s32[64]{0:T(128)} %left_ref.1) | copy-start | bytes 772
  2.1 36.7 %copy-start.6 = (s32[64]{0:T(128)S(1)}, s32[64]{0:T(128)}, u32[]{:S(2)}) copy-start(s32[64]{0:T(128)} %right_ref.1) | copy-start | bytes 772
  2.2 36.7 %copy-start.7 = (s32[64]{0:T(128)S(1)}, s32[64]{0:T(128)}, u32[]{:S(2)}) copy-start(s32[64]{0:T(128)} %aux_ref.1) | copy-start | bytes 772
  2.2 36.7 %copy-start.8 = (s32[64]{0:T(128)S(1)}, s32[64]{0:T(128)}, u32[]{:S(2)}) copy-start(s32[64]{0:T(128)} %dest_ref.1) | copy-start | bytes 772
  2.2 36.7 %all-to-all-start = ((bf16[8,64,8,128]{3,2,1,0:T(8,128)(2,1)}), bf16[8,64,8,128]{3,2,1,0:T(8,128)(2,1)S(1)}, u32[]{:S(2)}, u32[]{:S(2)}) async-start(bf16[8,64,8,128]{3,2,1,0:T(8,128)(2,1)} %broadcast_in_dim.3), calls=%async_computation | async-start | bytes 2097152 | tf_op jit(solution)/shard_map/all_to_all | solution.py:222
  37.7 1.1 %copy-start.1 = (bf16[12,256,256]{2,1,0:T(8,128)(2,1)}, bf16[12,256,256]{2,1,0:T(8,128)(2,1)S(1)}, u32[]{:S(2)}) copy-start(bf16[12,256,256]{2,1,0:T(8,128)(2,1)S(1)} %get-tuple-element.8.l_ref) | copy-start | bytes 4718596
  38.9 1.4 %copy-start.2 = (bf16[12,256,256]{2,1,0:T(8,128)(2,1)S(1)}, bf16[12,256,256]{2,1,0:T(8,128)(2,1)}, u32[]{:S(2)}) copy-start(bf16[12,256,256]{2,1,0:T(8,128)(2,1)} %copy-done.1) | copy-start | bytes 4718596

commit v2 on v0

v2 whole, which is shorter than its diff:
```python
import jax
import jax.numpy as jnp
from jax import lax
from jax.experimental import pallas as pl
from jax.experimental.pallas import tpu as pltpu
from jax.sharding import PartitionSpec as P

BF = jnp.bfloat16
F32 = jnp.float32
MB = 2**20
VM = pl.BlockSpec(memory_space=pltpu.VMEM)
SM = pl.BlockSpec(memory_space=pltpu.SMEM)
HB = pl.BlockSpec(memory_space=pltpu.HBM)
PEERS = 8
CORES = 2
HELD = 64


def iota(shape, dim):
    return lax.broadcasted_iota(jnp.int32, shape, dim)


def ones_where(mask):
    return jnp.where(mask, 1.0, 0.0).astype(BF)


def pack_kernel(d_ref, out_ref, flat_ref):
    blocks, cells = d_ref.shape
    d = d_ref[...]
    for b in range(cells // 256):
        col = iota((256, 256), 1) + b * 256
        source = (col % 32) * 32 + col // 32
        y = jnp.zeros((blocks, 256), F32)
        for a in range(cells // 256):
            move = ones_where(iota((256, 256), 0) + a * 256 == source)
            y += jnp.dot(d[:, a * 256:(a + 1) * 256], move, preferred_element_type=F32)
        for e in range(2):
            flat_ref[pl.ds(2 * b + e, blocks, stride=8), :] = y[:, e * 128:(e + 1) * 128]
    x = flat_ref[...].reshape(blocks, 8, 128).astype(BF)
    for p in range(out_ref.shape[0]):
        out_ref[p] = x


def run_pack(density, peers):
    blocks = density.shape[0]
    return pl.pallas_call(
        pack_kernel,
        out_shape=jax.ShapeDtypeStruct((peers, blocks, 8, 128), BF),
        in_specs=[VM],
        out_specs=VM,
        scratch_shapes=[pltpu.VMEM((blocks * 8, 128), F32)],
        compiler_params=pltpu.CompilerParams(vmem_limit_bytes=8 * MB),
    )(density)


def turned(x_ref, move_ref, top, tiles):
    z = jnp.dot(x_ref[top:top + tiles * 16, :], move_ref[...], preferred_element_type=F32)
    blocks = []
    for s in range(tiles):
        halves = []
        for h in range(2):
            row = (s * 2 + h) * 8
            halves.append(jnp.concatenate([z[row:row + 8, c * 128:(c + 1) * 128] for c in range(4)], axis=0))
        blocks.append(jnp.concatenate(halves, axis=1).astype(BF))
    return blocks


def prepare(me_ref, owner_ref, slot_ref, left_ref, right_ref, aux_ref, dest_ref, coeffs_ref, coulomb_ref,
            w_out, l_out, table_ref, names_ref, count_ref, y_ref, x_ref, move_ref, lw_ref, l_ref, w_ref, w_sem, l_sem):
    blocks, na, cells = coeffs_ref.shape
    vrows = coulomb_ref.shape[0]
    aux = vrows // na
    tiles = na // 8
    tasks = slot_ref.shape[0]
    share = tasks // blocks
    peers, cap = PEERS, 128 // PEERS
    sub, lane = iota((8, 128), 0), iota((8, 128), 1)
    me = me_ref[0]
    for b in range(blocks + peers):
        count_ref[b] = 0

    def count_some(r):
        for u in range(share):
            right = right_ref[r * share + u]
            count_ref[right] = count_ref[right] + 1

    def place_some(r, names):
        for u in range(share):
            t = r * share + u
            right = right_ref[t]
            spot = count_ref[right]
            count_ref[right] = spot + 1
            dest = dest_ref[t]
            peer = lax.rem(dest, peers)
            place = count_ref[blocks + peer]
            count_ref[blocks + peer] = place + 1
            owner = owner_ref[t]
            table_ref[spot] = lax.rem(owner, CORES) * (HELD * peers // CORES) + owner // CORES * HELD + slot_ref[t]
            table_ref[tasks + spot] = right * aux + aux_ref[t]
            table_ref[2 * tasks + spot] = left_ref[t]
            table_ref[3 * tasks + spot] = peer * (cap + 1) + place
            table_ref[4 * tasks + spot] = right
            name = (dest // peers + 1).astype(F32)
            names = jnp.where((sub == peer) & (lane == me * cap + place), name, names)
        return names

    row, col = iota((512, 512), 0), iota((512, 512), 1)
    move_ref[...] = ones_where(row == (col % 128) // 32 * 128 + col // 128 * 32 + col % 32)

    def store(full, q, count):
        for e in range(2):
            v = 2 * q + e
            for mt in range(count):
                y_ref[mt * 64 + v * 8:mt * 64 + v * 8 + 8, :] = full[mt * 8:mt * 8 + 8, e * 128:(e + 1) * 128]

    def gather(count):
        for mt in range(count):
            for m in range(4):
                pair = [y_ref[pl.ds(mt * 64 + 4 * h + m, 8, stride=8), :] for h in range(2)]
                x_ref[mt * 16:(mt + 1) * 16, m * 128:(m + 1) * 128] = jnp.concatenate(pair, axis=0).astype(BF)

    def one_left(r, carry):
        for q in range(cells // 256):
            store(coeffs_ref[r, :, q * 256:(q + 1) * 256].astype(F32), q, tiles)
        gather(tiles)
        for s, block in enumerate(turned(x_ref, move_ref, 0, tiles)):
            lw_ref[s, pl.ds(pl.multiple_of(r * 32, 32), 32), :] = block
        count_some(r)
        return carry

    lax.fori_loop(0, blocks, one_left, 0, unroll=4)
    first = 0
    for r in range(blocks):
        many = count_ref[r]
        count_ref[r] = first
        first = first + many
    for s in range(tiles):
        l_ref[s * 256:(s + 1) * 256, :] = jnp.transpose(lw_ref[s])
    l_copy = pltpu.make_async_copy(l_ref, l_out, l_sem)
    l_copy.start()

    def w_copy(r):
        part = pl.ds(r * aux, aux)
        return pltpu.make_async_copy(w_ref.at[part], w_out.at[part], w_sem.at[r])

    def one(r, names):
        vall = coulomb_ref[...]
        for q in range(cells // 256):
            store(jnp.dot(vall, coeffs_ref[r, :, q * 256:(q + 1) * 256], preferred_element_type=F32), q, aux * tiles)
        gather(aux * tiles)
        for a in range(aux):
            for s, block in enumerate(turned(x_ref, move_ref, a * tiles * 16, tiles)):
                w_ref[r * aux + a, s * 32:(s + 1) * 32, :] = block
        w_copy(r).start()
        return place_some(r, names)

    names_ref[...] = lax.fori_loop(0, blocks, one, jnp.zeros((8, 128), F32), unroll=2)
    for r in range(blocks):
        w_copy(r).wait()
    l_copy.wait()


def run_prepare(me, owner, slot, left, right, aux_of, dest, coeffs, vall):
    blocks, na, cells = coeffs.shape
    aux = vall.shape[0] // na
    tiles = na // 8
    rows = vall.shape[0] + na
    return pl.pallas_call(
        prepare,
        out_shape=(
            pltpu.HBM((blocks * aux, tiles * 32, 256), BF),
            pltpu.HBM((tiles * 256, blocks * 32), BF),
            jax.ShapeDtypeStruct((1024,), jnp.int32),
            jax.ShapeDtypeStruct((8, 128), F32),
        ),
        in_specs=[SM] * 7 + [VM, VM],
        out_specs=(HB, HB, SM, VM),
        scratch_shapes=[
            pltpu.SMEM((blocks + PEERS,), jnp.int32),
            pltpu.VMEM((rows * 8, 128), F32),
            pltpu.VMEM((rows * 2, 512), BF),
            pltpu.VMEM((512, 512), BF),
            pltpu.VMEM((tiles, blocks * 32, 256), BF),
            pltpu.VMEM((tiles * 256, blocks * 32), BF),
            pltpu.VMEM((blocks * aux, tiles * 32, 256), BF),
            pltpu.SemaphoreType.DMA((blocks,)),
            pltpu.SemaphoreType.DMA,
        ],
        compiler_params=pltpu.CompilerParams(vmem_limit_bytes=24 * MB),
    )(me, owner, slot, left, right, aux_of, dest, coeffs, vall)


def tasks_kernel(table_ref, names_ref, w_in, l_in, d_ref,
                 out_ref, dl_ref, a0_ref, a1_ref, send_ref, w_ref, l_ref, w_sem, l_sem):
    tiles = l_ref.shape[0] // 256
    lefts = l_ref.shape[1] // 32
    aux = w_ref.shape[0] // lefts
    tasks = dl_ref.shape[0] // 32
    groups = tasks // 8
    slots = out_ref.shape[1]

    def w_copy(r):
        part = pl.ds(r * aux, aux)
        return pltpu.make_async_copy(w_in.at[part], w_ref.at[part], w_sem.at[r])

    l_copy = pltpu.make_async_copy(l_in, l_ref, l_sem)
    w_copy(0).start()
    l_copy.start()
    for r in range(1, lefts):
        w_copy(r).start()
    send_ref[...] = jnp.zeros_like(send_ref)

    spread = ones_where(iota((256, 64), 0) // 4 == iota((256, 64), 1))
    own_chunk = iota((256, 128), 0) % 4 == iota((256, 128), 1) // 32
    repeat = ones_where(iota((128, 256), 0) % 32 == iota((128, 256), 1) % 32)
    for g in range(groups):
        picked = [d_ref[table_ref[g * 8 + u]].astype(F32) for u in range(8)]
        e = jnp.dot(spread, jnp.concatenate(picked, axis=0).astype(BF), preferred_element_type=F32)
        e = jnp.where(own_chunk, e, 0.0).astype(BF)
        dl_ref[g * 256:(g + 1) * 256, :] = jnp.dot(e, repeat, preferred_element_type=F32).astype(BF)

    diag = ones_where(iota((256, 256), 0) // 32 == iota((256, 256), 1) // 32)
    fold = ones_where(iota((256, 128), 0) % 32 == iota((256, 128), 1) % 32)
    chunk = iota((8, 128), 1) // 32
    column = iota((32, 256), 1) // 32

    def apply(g, a_ref):
        for u in range(8):
            d = dl_ref[pl.ds(pl.multiple_of(g * 256 + u * 32, 32), 32), :]
            bd = jnp.concatenate([d] * 8, axis=0) * diag
            w = w_ref[table_ref[tasks + g * 8 + u]]
            y = jnp.dot(w, bd, preferred_element_type=F32).astype(BF)
            for s in range(tiles):
                a_ref[u * 32:(u + 1) * 32, s * 256:(s + 1) * 256] = y[s * 32:(s + 1) * 32, :]

    def close(g, a_ref):
        total = jnp.dot(a_ref[...], l_ref[...], preferred_element_type=F32)
        own = [jnp.where(column == table_ref[2 * tasks + g * 8 + u], total[u * 32:(u + 1) * 32, :], 0.0) for u in range(8)]
        total = jnp.dot(jnp.concatenate(own, axis=0).astype(BF), fold, preferred_element_type=F32)
        for u in range(8):
            block = total[u * 32:u * 32 + 8, :]
            for q in range(1, 4):
                block = jnp.where(chunk == q, total[u * 32 + q * 8:u * 32 + q * 8 + 8, :], block)
            send_ref[table_ref[3 * tasks + g * 8 + u]] = block

    def wait_to(g, waited):
        last = table_ref[4 * tasks + g * 8 + 7] + 1

        def wait(r, c):
            w_copy(r).wait()
            return c

        lax.fori_loop(waited, last, wait, 0)
        return jnp.maximum(waited, last)

    waited = wait_to(0, jnp.int32(0))
    apply(0, a0_ref)
    l_copy.wait()

    def two(h, waited):
        waited = wait_to(2 * h + 2, waited)
        apply(2 * h + 1, a1_ref)
        close(2 * h, a0_ref)
        apply(2 * h + 2, a0_ref)
        close(2 * h + 1, a1_ref)
        return waited

    waited = lax.fori_loop(0, groups // 2 - 1, two, waited)
    waited = wait_to(groups - 1, waited)
    apply(groups - 1, a1_ref)
    close(groups - 2, a0_ref)
    close(groups - 1, a1_ref)

    def drain(r, c):
        w_copy(r).wait()
        return c

    lax.fori_loop(waited, lefts, drain, 0)
    names = names_ref[...]
    for p in range(out_ref.shape[0]):
        send_ref[p * slots + slots - 1] = jnp.broadcast_to(names[p:p + 1, :], (8, 128))
    out_ref[...] = send_ref[...].reshape(out_ref.shape).astype(out_ref.dtype)


def run_tasks(table, names, w, l, dens, tasks, peers, cap):
    w = pltpu.with_memory_space_constraint(w, pltpu.HBM)
    l = pltpu.with_memory_space_constraint(l, pltpu.HBM)
    return pl.pallas_call(
        tasks_kernel,
        out_shape=jax.ShapeDtypeStruct((peers, cap + 1, 8, 128), BF),
        in_specs=[SM, VM, HB, HB, VM],
        out_specs=VM,
        scratch_shapes=[
            pltpu.VMEM((tasks * 32, 256), BF),
            pltpu.VMEM((256, l.shape[0]), BF),
            pltpu.VMEM((256, l.shape[0]), BF),
            pltpu.VMEM((peers * (cap + 1), 8, 128), F32),
            pltpu.VMEM(w.shape, BF),
            pltpu.VMEM(l.shape, BF),
            pltpu.SemaphoreType.DMA((l.shape[1] // 32,)),
            pltpu.SemaphoreType.DMA,
        ],
        compiler_params=pltpu.CompilerParams(vmem_limit_bytes=24 * MB),
    )(table, names, w, l, dens)


def spread_kernel(recv_ref, out_ref, flat_ref):
    peers, slots = recv_ref.shape[0], recv_ref.shape[1]
    cap = slots - 1
    rows = out_ref.shape[0]
    names = recv_ref[0, cap].astype(F32)
    for p in range(1, peers):
        names = names + recv_ref[p, cap].astype(F32)
    names = jnp.broadcast_to(names[0:1, :], (rows, 128)).astype(jnp.int32)
    hot = ones_where(iota((rows, 128), 0) + 1 == names)
    for p in range(peers):
        for n in range(cap):
            flat_ref[(p * cap + n) * 8:(p * cap + n + 1) * 8, :] = recv_ref[p, n].astype(F32)
    sums = []
    for i in range(8):
        x = flat_ref[pl.ds(i, 128, stride=8), :]
        sums.append(jnp.dot(hot, x.astype(BF), preferred_element_type=F32))
    for i in range(8):
        flat_ref[pl.ds(i, rows, stride=8), :] = sums[i]
    out_ref[...] = flat_ref[0:rows * 8, :].reshape(rows, 8, 128).astype(out_ref.dtype)


def run_spread(recv, rows, dtype):
    peers, slots = recv.shape[:2]
    return pl.pallas_call(
        spread_kernel,
        out_shape=jax.ShapeDtypeStruct((rows, 8, 128), dtype),
        in_specs=[VM],
        out_specs=VM,
        scratch_shapes=[pltpu.VMEM((max(rows, peers * (slots - 1)) * 8, 128), F32)],
        compiler_params=pltpu.CompilerParams(vmem_limit_bytes=8 * MB),
    )(recv)


def exact_dot(x, y):
    out = None
    for _ in range(3):
        part = x.astype(BF)
        x = x - part.astype(F32)
        term = jnp.dot(part, y, preferred_element_type=F32)
        out = term if out is None else out + term
    return out


def final_kernel(recv_ref, out_ref):
    total = jnp.sum(recv_ref[...].astype(F32), axis=0) * -0.25
    vi = iota((64, 128), 0) // 8
    wide = jnp.concatenate([total] * 8, axis=0)
    wide = jnp.where(iota((64, 128), 1) % 8 == vi, wide, 0.0)
    r, c = iota((128, 128), 0), iota((128, 128), 1)
    move = ones_where((r // 32 == c % 4) & (r % 32 // 8 == c // 32))
    wide = exact_dot(wide, move)
    wide = jnp.where(iota((64, 128), 1) % 32 // 4 == iota((64, 128), 0) % 8, wide, 0.0)
    out_ref[...] = jnp.sum(wide.reshape(8, 8, 128), axis=1)


def run_final(recv):
    return pl.pallas_call(
        final_kernel,
        out_shape=jax.ShapeDtypeStruct((8, 128), F32),
        in_specs=[VM],
        out_specs=VM,
        compiler_params=pltpu.CompilerParams(vmem_limit_bytes=4 * MB),
    )(recv)


def per_device(coeffs, coulomb, density, task_owner, task_slot, task_left, task_right, task_aux, task_dest):
    na = coeffs.shape[1]
    blk, task = lax.axis_size("blk"), lax.axis_size("task")
    chips = blk // CORES
    same_core = [[x * CORES + c for x in range(chips)] for c in range(CORES)]
    same_chip = [[x * CORES + c for c in range(CORES)] for x in range(chips)]
    dens = lax.all_to_all(run_pack(density, chips), "blk", 0, 0, tiled=True, axis_index_groups=same_core)
    me = lax.axis_index("blk").astype(jnp.int32).reshape(1)
    w, l, table, names = run_prepare(me, task_owner.reshape(-1), task_slot, task_left, task_right, task_aux, task_dest,
                                     coeffs, coulomb.reshape(coulomb.shape[0] * na, na))
    dens = lax.all_gather(dens.reshape(chips * HELD, 8, 128), "blk", axis=0, tiled=True, axis_index_groups=same_chip)
    send = run_tasks(table, names, w, l, dens, task_slot.shape[0], blk, 128 // blk)
    recv = lax.all_to_all(send, "blk", 0, 0, tiled=True)
    rows = run_spread(recv, task, BF)
    back = lax.all_to_all(rows, "task", 0, 0, tiled=True)
    return run_final(back).reshape(1, density.shape[1])


def solution(mesh):
    every = P(("task", "blk"))
    placed = (every, every, P("blk"), every, every, every, every, every, every)
    return jax.shard_map(per_device, mesh=mesh, in_specs=placed, out_specs=every, check_vma=False)
```

time: 691 us -> 115 us (0.17)
  waiting for transfers between devices: 522 us -> 18.2 us
  local copies, waits for them, and re-layouts: 97.8 us -> 2.4 us
  blocking collectives: 0 us -> 53.6 us
  matrix products: 49.1 us -> 0 us
  Pallas kernels: 0 us -> 26.2 us
    unnamed x3 -> x1, waiting for transfers between devices: 485 us -> 0.02 us
    gather x41 -> x0, local copies, waits for them, and re-layouts: 92 us -> none  [the longest x16 49.2 us: group_work(): coeffs[right_rows].reshape(group_size, na_count, no_side, no_side)]
    all_to_all x0 -> x3, blocking collectives: none -> 53.6 us  [the longest x1 32.1 us: per_device(): back = lax.all_to_all(rows, 'task', 0, 0, tiled=True)]
    dot_general x16 -> x0, matrix products: 49.1 us -> none  [the longest x8 32.9 us: group_work(): jnp.einsum('tmik,tmjk->tij', left_blocks, applied, preferred_element_type...]
    pallas_call x0 -> x5, Pallas kernels: none -> 26.2 us  [the longest x1 12.9 us: run_tasks(): pl.pallas_call(tasks_kernel, out_shape=jax.ShapeDtypeStruct((peers, cap +...]
    all_gather x1, waiting for transfers between devices: 37.8 us -> 18.2 us  [per_device(): lax.all_gather(dens.reshape(chips * HELD, 8, 128), 'blk', axis=0, tiled=T...]
  transfers between devices with their start and end apart: 2 -> 1, of which waited for: 2 -> 1; matrix products, arithmetic and copies ran while one was open for 1% -> 0% of each run, Pallas kernels for 0% -> 10%
where the time goes in v2:
time: 115 us; the launch traced here: 114 us
  blocking collectives  53.6 us (47%)
  Pallas kernels  26.2 us (23%)
  waiting for transfers between devices  18.2 us (16%)
  between operations  13.5 us (12%)
  local copies, waits for them, and re-layouts  2.4 us (2%)
    all_to_all x1, blocking collectives, per_device(): back = lax.all_to_all(rows, 'task', 0, 0, tiled=True)  32.1 us
    all_gather x1, waiting for transfers between devices, per_device(): lax.all_gather(dens.reshape(chips * HELD, 8, 128), 'blk', axis=0, tiled=T...  18.2 us
    pallas_call x1, Pallas kernels, run_tasks(): pl.pallas_call(tasks_kernel, out_shape=jax.ShapeDtypeStruct((peers, cap +...  12.9 us
    all_to_all x1, blocking collectives, per_device(): lax.all_to_all(run_pack(density, chips), 'blk', 0, 0, tiled=True, axis_in...  11.7 us
    pallas_call x1, Pallas kernels, run_prepare(): pl.pallas_call(prepare, out_shape=(pltpu.HBM((blocks * aux, tiles * 32, 2...  11.5 us
    all_to_all x1, blocking collectives, per_device(): recv = lax.all_to_all(send, 'blk', 0, 0, tiled=True)  9.83 us
  transfers between devices with their start and end apart: 1, of which 1 were waited for; matrix products, arithmetic and copies ran while one was open for 0% of the time, Pallas kernels for 10%

profile of v2, /device:TPU:1, one launch (start us, length us, event | category | flops | bytes accessed | tf_op | source)
XLA Modules:
  0.0 113.9 jit_solution(13691979419469142141)
XLA Ops:
  6.5 0.0 copy-start
  6.5 0.0 all-gather.2.cloned.1.call-start
  6.5 0.0 copy-start.2
  6.5 1.0 copy-done.2
  7.6 0.0 copy-start.9
  7.6 0.0 copy-start.3
  7.6 0.0 copy-start.4
  7.6 0.0 copy-start.5
  7.6 0.0 copy-start.6
  7.6 0.0 copy-start.7
  7.6 0.0 copy-start.8
  7.6 0.5 shard_map.92
  8.2 11.7 %all_to_all.15 = bf16[4,64,8,128]{3,2,1,0:T(8,128)(2,1)} all-to-all(bf16[4,64,8,128]{3,2,1,0:T(8,128)(2,1)S(1)} %shard_map.92), channel_id=1, replica_groups={{0,2,4,6},{1,3,5,7},{8,10,12,14},{9,11,13,15},{16,18,20,22},{17,19,21,2..., dimensions={0} | all-to-all | bytes 1048576 | tf_op jit(solution)/shard_map/all_to_all | solution.py:378
  19.8 0.0 all-gather.2.cloned.1.call-update
  19.9 0.0 copy-done.9
  19.9 0.1 reshape.17.coulomb_ref
  20.0 0.0 copy-done
  20.0 0.0 copy-done.3
  20.0 0.0 copy-done.4
  20.0 0.0 copy-done.5
  20.0 0.0 copy-done.6
  20.1 0.0 copy-done.7
  20.1 0.0 copy-done.8
  20.1 11.5 %shard_map.91 = (bf16[32,384,256]{2,1,0:T(8,128)(2,1)}, bf16[3072,256]{1,0:T(8,128)(2,1)}, s32[1024]{0:T(1024)S(1)}, f32[8,128]{1,0:T(8,128)S(1)}) custom-call(s32[1]{0:T(128)} %bitcast.me_ref, s32[64]{0:T(128)S(1)} %bitcast.4, s32[64]{0:T(128)S(1)} %copy-done.4, s32[64]{0:T(128)S(1)} %copy-done.5, s32[64]{0:T(128)S(1)} %copy-done.6, s32[64]{0:T(128)S(1)} %copy-done.7, ...), custom_call_target="tpu_custom_call" | custom-call | tf_op jit(solution)/shard_map/pallas_call | solution.py:168
  31.6 18.2 %all-gather.2.cloned.1.call-done.d_ref = bf16[512,8,128]{2,1,0:T(8,128)(2,1)} async-done(((bf16[256,8,128]{2,1,0:T(8,128)(2,1)}), bf16[512,8,128]{2,1,0:T(8,128)(2,1)}) %all-gather.2.cloned.1.call-update) | async-done | bytes 1048592 | tf_op jit(solution)/shard_map/all_gather | solution.py:382
  49.8 0.0 copy-start.1
  49.8 1.2 %copy-done.1 = bf16[512,8,128]{2,1,0:T(8,128)(2,1)S(1)} copy-done((bf16[512,8,128]{2,1,0:T(8,128)(2,1)S(1)}, bf16[512,8,128]{2,1,0:T(8,128)(2,1)}, u32[]{:S(2)}) %copy-start.1) | copy-done | bytes 1048600
  51.0 12.9 %shard_map.93 = bf16[8,17,8,128]{3,2,1,0:T(8,128)(2,1)S(1)} custom-call(s32[1024]{0:T(1024)S(1)} %get-tuple-element.9.table_ref, f32[8,128]{1,0:T(8,128)S(1)} %get-tuple-element.10.names_ref, bf16[32,384,256]{2,1,0:T(8,128)(2,1)} %get-tuple-element.11.w_in, bf16[3072,256]{1,0:T(8,128)(2,1)} %get-tuple-element.12.l_in, bf16[512,8,128]{2,1,0:T(8,128)(2,1)S(1)} %copy-done.1), custom_call_target="tpu_custom_call" | custom-call | tf_op jit(solution)/shard_map/pallas_call | solution.py:288
  64.0 9.8 %all_to_all.16.recv_ref = bf16[8,17,8,128]{3,2,1,0:T(8,128)(2,1)S(1)} all-to-all(bf16[8,17,8,128]{3,2,1,0:T(8,128)(2,1)S(1)} %shard_map.93), channel_id=1, replica_groups=mesh['task'=96,'blk'=8] {'blk'}, dimensions={0} | all-to-all | bytes 557056 | tf_op jit(solution)/shard_map/all_to_all | solution.py:384
  73.8 0.3 shard_map.94
  74.1 32.1 %all_to_all.17.recv_ref = bf16[96,8,128]{2,1,0:T(8,128)(2,1)S(1)} all-to-all(bf16[96,8,128]{2,1,0:T(8,128)(2,1)S(1)} %shard_map.94), channel_id=1, replica_groups=mesh['task'=96,'blk'=8] {'task'}, dimensions={0} | all-to-all | bytes 393216 | tf_op jit(solution)/shard_map/all_to_all | solution.py:386
  106.2 0.9 shard_map.95
Async XLA Ops:
  6.5 13.5 %copy-start = (bf16[8,96,1024]{2,1,0:T(8,128)(2,1)S(1)}, bf16[8,96,1024]{2,1,0:T(8,128)(2,1)}, u32[]{:S(2)}) copy-start(bf16[8,96,1024]{2,1,0:T(8,128)(2,1)} %coeffs_ref.1) | copy-start | bytes 4718596
  6.5 43.3 %all-gather.2.cloned.1.call-start = ((), (), s32[]{:S(2)}) async-start(), calls=%async_computation.3 | async-start | bytes 1572864 | tf_op jit(solution)/shard_map/all_gather | solution.py:382
  6.5 1.0 copy-start.2
  7.6 12.3 %copy-start.9 = (bf16[4,9216]{1,0:T(4,128)(2,1)S(1)}, bf16[4,9216]{1,0:T(4,128)(2,1)}, u32[]{:S(2)}) copy-start(bf16[4,9216]{1,0:T(4,128)(2,1)} %param.10) | copy-start | bytes 221188
  7.6 12.5 %copy-start.3 = (s32[64,1]{0,1:T(1,128)S(1)}, s32[64,1]{0,1:T(1,128)}, u32[]{:S(2)}) copy-start(s32[64,1]{0,1:T(1,128)} %param.12) | copy-start | bytes 772
  7.6 12.5 %copy-start.4 = (s32[64]{0:T(128)S(1)}, s32[64]{0:T(128)}, u32[]{:S(2)}) copy-start(s32[64]{0:T(128)} %slot_ref.1) | copy-start | bytes 772
  7.6 12.5 %copy-start.5 = (s32[64]{0:T(128)S(1)}, s32[64]{0:T(128)}, u32[]{:S(2)}) copy-start(s32[64]{0:T(128)} %left_ref.1) | copy-start | bytes 772
  7.6 12.5 %copy-start.6 = (s32[64]{0:T(128)S(1)}, s32[64]{0:T(128)}, u32[]{:S(2)}) copy-start(s32[64]{0:T(128)} %right_ref.1) | copy-start | bytes 772
  7.6 12.5 %copy-start.7 = (s32[64]{0:T(128)S(1)}, s32[64]{0:T(128)}, u32[]{:S(2)}) copy-start(s32[64]{0:T(128)} %aux_ref.1) | copy-start | bytes 772
  7.6 12.5 %copy-start.8 = (s32[64]{0:T(128)S(1)}, s32[64]{0:T(128)}, u32[]{:S(2)}) copy-start(s32[64]{0:T(128)} %dest_ref.1) | copy-start | bytes 772
  49.8 1.2 %copy-start.1 = (bf16[512,8,128]{2,1,0:T(8,128)(2,1)S(1)}, bf16[512,8,128]{2,1,0:T(8,128)(2,1)}, u32[]{:S(2)}) copy-start(bf16[512,8,128]{2,1,0:T(8,128)(2,1)} %all-gather.2.cloned.1.call-done.d_ref) | copy-start | bytes 3145732
Sparse Core Ops, SparseCore 0:
  20.0 29.7 all-gather.1

commit v3 on v2

--- a/solution.py
+++ b/solution.py
@@ -14,6 +14,7 @@
 PEERS = 8
 CORES = 2
 HELD = 64
+AUX = 4
 
 
 def iota(shape, dim):
@@ -53,8 +54,27 @@
     )(density)
 
 
-def turned(x_ref, move_ref, top, tiles):
-    z = jnp.dot(x_ref[top:top + tiles * 16, :], move_ref[...], preferred_element_type=F32)
+def lane_move():
+    row, col = iota((512, 512), 0), iota((512, 512), 1)
+    return ones_where(row == (col % 128) // 32 * 128 + col // 128 * 32 + col % 32)
+
+
+def put_rows(y_ref, full, q, count):
+    for e in range(2):
+        v = 2 * q + e
+        for mt in range(count):
+            y_ref[mt * 64 + v * 8:mt * 64 + v * 8 + 8, :] = full[mt * 8:mt * 8 + 8, e * 128:(e + 1) * 128]
+
+
+def gather_rows(y_ref, x_ref, first, count):
+    for mt in range(first, first + count):
+        for m in range(4):
+            pair = [y_ref[pl.ds(mt * 64 + 4 * h + m, 8, stride=8), :] for h in range(2)]
+            x_ref[mt * 16:(mt + 1) * 16, m * 128:(m + 1) * 128] = jnp.concatenate(pair, axis=0).astype(BF)
+
+
+def turned(x_ref, move_ref, first, tiles):
+    z = jnp.dot(x_ref[first * 16:(first + tiles) * 16, :], move_ref[...], preferred_element_type=F32)
     blocks = []
     for s in range(tiles):
         halves = []
@@ -65,11 +85,9 @@
     return blocks
 
 
-def prepare(me_ref, owner_ref, slot_ref, left_ref, right_ref, aux_ref, dest_ref, coeffs_ref, coulomb_ref,
-            w_out, l_out, table_ref, names_ref, count_ref, y_ref, x_ref, move_ref, lw_ref, l_ref, w_ref, w_sem, l_sem):
+def lefts_kernel(me_ref, owner_ref, slot_ref, left_ref, right_ref, aux_ref, dest_ref, coeffs_ref,
+                 l_out, table_ref, names_ref, count_ref, y0_ref, y1_ref, x0_ref, x1_ref, move_ref, lw_ref, l_ref, l_sem):
     blocks, na, cells = coeffs_ref.shape
-    vrows = coulomb_ref.shape[0]
-    aux = vrows // na
     tiles = na // 8
     tasks = slot_ref.shape[0]
     share = tasks // blocks
@@ -78,6 +96,7 @@
     me = me_ref[0]
     for b in range(blocks + peers):
         count_ref[b] = 0
+    move_ref[...] = lane_move()
 
     def count_some(r):
         for u in range(share):
@@ -95,8 +114,8 @@
             place = count_ref[blocks + peer]
             count_ref[blocks + peer] = place + 1
             owner = owner_ref[t]
-            table_ref[spot] = lax.rem(owner, CORES) * (HELD * peers // CORES) + owner // CORES * HELD + slot_ref[t]
-            table_ref[tasks + spot] = right * aux + aux_ref[t]
+            table_ref[spot] = lax.rem(owner + me, CORES) * (HELD * peers // CORES) + owner // CORES * HELD + slot_ref[t]
+            table_ref[tasks + spot] = right * AUX + aux_ref[t]
             table_ref[2 * tasks + spot] = left_ref[t]
             table_ref[3 * tasks + spot] = peer * (cap + 1) + place
             table_ref[4 * tasks + spot] = right
@@ -104,93 +123,121 @@
             names = jnp.where((sub == peer) & (lane == me * cap + place), name, names)
         return names
 
-    row, col = iota((512, 512), 0), iota((512, 512), 1)
-    move_ref[...] = ones_where(row == (col % 128) // 32 * 128 + col // 128 * 32 + col % 32)
-
-    def store(full, q, count):
-        for e in range(2):
-            v = 2 * q + e
-            for mt in range(count):
-                y_ref[mt * 64 + v * 8:mt * 64 + v * 8 + 8, :] = full[mt * 8:mt * 8 + 8, e * 128:(e + 1) * 128]
-
-    def gather(count):
-        for mt in range(count):
-            for m in range(4):
-                pair = [y_ref[pl.ds(mt * 64 + 4 * h + m, 8, stride=8), :] for h in range(2)]
-                x_ref[mt * 16:(mt + 1) * 16, m * 128:(m + 1) * 128] = jnp.concatenate(pair, axis=0).astype(BF)
-
-    def one_left(r, carry):
-        for q in range(cells // 256):
-            store(coeffs_ref[r, :, q * 256:(q + 1) * 256].astype(F32), q, tiles)
-        gather(tiles)
-        for s, block in enumerate(turned(x_ref, move_ref, 0, tiles)):
-            lw_ref[s, pl.ds(pl.multiple_of(r * 32, 32), 32), :] = block
+    for r in range(blocks):
         count_some(r)
-        return carry
-
-    lax.fori_loop(0, blocks, one_left, 0, unroll=4)
     first = 0
     for r in range(blocks):
         many = count_ref[r]
         count_ref[r] = first
         first = first + many
+
+    def two(h, names):
+        for e, (y_ref, x_ref) in enumerate(((y0_ref, x0_ref), (y1_ref, x1_ref))):
+            r = 2 * h + e
+            for q in range(cells // 256):
+                put_rows(y_ref, coeffs_ref[r, :, q * 256:(q + 1) * 256].astype(F32), q, tiles)
+            gather_rows(y_ref, x_ref, 0, tiles)
+            for s, block in enumerate(turned(x_ref, move_ref, 0, tiles)):
+                lw_ref[s, pl.ds(pl.multiple_of(r * 32, 32), 32), :] = block
+            names = place_some(r, names)
+        return names
+
+    names_ref[...] = lax.fori_loop(0, blocks // 2, two, jnp.zeros((8, 128), F32), unroll=2)
     for s in range(tiles):
         l_ref[s * 256:(s + 1) * 256, :] = jnp.transpose(lw_ref[s])
     l_copy = pltpu.make_async_copy(l_ref, l_out, l_sem)
     l_copy.start()
-
-    def w_copy(r):
-        part = pl.ds(r * aux, aux)
-        return pltpu.make_async_copy(w_ref.at[part], w_out.at[part], w_sem.at[r])
-
-    def one(r, names):
-        vall = coulomb_ref[...]
-        for q in range(cells // 256):
-            store(jnp.dot(vall, coeffs_ref[r, :, q * 256:(q + 1) * 256], preferred_element_type=F32), q, aux * tiles)
-        gather(aux * tiles)
-        for a in range(aux):
-            for s, block in enumerate(turned(x_ref, move_ref, a * tiles * 16, tiles)):
-                w_ref[r * aux + a, s * 32:(s + 1) * 32, :] = block
-        w_copy(r).start()
-        return place_some(r, names)
-
-    names_ref[...] = lax.fori_loop(0, blocks, one, jnp.zeros((8, 128), F32), unroll=2)
-    for r in range(blocks):
-        w_copy(r).wait()
     l_copy.wait()
 
 
-def run_prepare(me, owner, slot, left, right, aux_of, dest, coeffs, vall):
+def run_lefts(me, owner, slot, left, right, aux_of, dest, coeffs):
     blocks, na, cells = coeffs.shape
-    aux = vall.shape[0] // na
     tiles = na // 8
-    rows = vall.shape[0] + na
-    return pl.pallas_call(
-        prepare,
+    return pl.pallas_call(
+        lefts_kernel,
         out_shape=(
-            pltpu.HBM((blocks * aux, tiles * 32, 256), BF),
             pltpu.HBM((tiles * 256, blocks * 32), BF),
             jax.ShapeDtypeStruct((1024,), jnp.int32),
             jax.ShapeDtypeStruct((8, 128), F32),
         ),
-        in_specs=[SM] * 7 + [VM, VM],
-        out_specs=(HB, HB, SM, VM),
+        in_specs=[SM] * 7 + [VM],
+        out_specs=(HB, SM, VM),
         scratch_shapes=[
             pltpu.SMEM((blocks + PEERS,), jnp.int32),
-            pltpu.VMEM((rows * 8, 128), F32),
-            pltpu.VMEM((rows * 2, 512), BF),
+            pltpu.VMEM((na * 8, 128), F32),
+            pltpu.VMEM((na * 8, 128), F32),
+            pltpu.VMEM((na * 2, 512), BF),
+            pltpu.VMEM((na * 2, 512), BF),
             pltpu.VMEM((512, 512), BF),
             pltpu.VMEM((tiles, blocks * 32, 256), BF),
             pltpu.VMEM((tiles * 256, blocks * 32), BF),
+            pltpu.SemaphoreType.DMA,
+        ],
+        compiler_params=pltpu.CompilerParams(vmem_limit_bytes=16 * MB),
+    )(me, owner, slot, left, right, aux_of, dest, coeffs)
+
+
+def rights_kernel(coeffs_ref, coulomb_ref, after_ref, w_out, y0_ref, y1_ref, x0_ref, x1_ref, move_ref, w_ref, w_sem):
+    blocks, na, cells = coeffs_ref.shape
+    vrows = coulomb_ref.shape[0]
+    aux = vrows // na
+    tiles = na // 8
+    move_ref[...] = lane_move()
+
+    def w_copy(r):
+        part = pl.ds(r * aux, aux)
+        return pltpu.make_async_copy(w_ref.at[part], w_out.at[part], w_sem.at[r])
+
+    def multiply(r, y_ref):
+        for q in range(cells // 256):
+            y = jnp.dot(coulomb_ref[...], coeffs_ref[r, :, q * 256:(q + 1) * 256], preferred_element_type=F32)
+            put_rows(y_ref, y, q, aux * tiles)
+
+    def turn(r, y_ref, x_ref):
+        for a in range(aux):
+            gather_rows(y_ref, x_ref, a * tiles, tiles)
+            for s, block in enumerate(turned(x_ref, move_ref, a * tiles, tiles)):
+                w_ref[r * aux + a, s * 32:(s + 1) * 32, :] = block
+        w_copy(r).start()
+
+    multiply(0, y0_ref)
+
+    def two(h, carry):
+        multiply(2 * h + 1, y1_ref)
+        turn(2 * h, y0_ref, x0_ref)
+        multiply(jnp.minimum(2 * h + 2, blocks - 1), y0_ref)
+        turn(2 * h + 1, y1_ref, x1_ref)
+        return carry
+
+    lax.fori_loop(0, blocks // 2, two, 0)
+    for r in range(blocks):
+        w_copy(r).wait()
+
+
+def run_rights(coeffs, vall, after):
+    blocks, na, cells = coeffs.shape
+    aux = vall.shape[0] // na
+    tiles = na // 8
+    rows = vall.shape[0]
+    return pl.pallas_call(
+        rights_kernel,
+        out_shape=pltpu.HBM((blocks * aux, tiles * 32, 256), BF),
+        in_specs=[VM, VM, pl.BlockSpec(memory_space=pl.ANY)],
+        out_specs=HB,
+        scratch_shapes=[
+            pltpu.VMEM((rows * 8, 128), F32),
+            pltpu.VMEM((rows * 8, 128), F32),
+            pltpu.VMEM((rows * 2, 512), BF),
+            pltpu.VMEM((rows * 2, 512), BF),
+            pltpu.VMEM((512, 512), BF),
             pltpu.VMEM((blocks * aux, tiles * 32, 256), BF),
             pltpu.SemaphoreType.DMA((blocks,)),
-            pltpu.SemaphoreType.DMA,
         ],
         compiler_params=pltpu.CompilerParams(vmem_limit_bytes=24 * MB),
-    )(me, owner, slot, left, right, aux_of, dest, coeffs, vall)
-
-
-def tasks_kernel(table_ref, names_ref, w_in, l_in, d_ref,
+    )(coeffs, vall, after)
+
+
+def tasks_kernel(table_ref, names_ref, w_in, l_in, d_ref, e_ref,
                  out_ref, dl_ref, a0_ref, a1_ref, send_ref, w_ref, l_ref, w_sem, l_sem):
     tiles = l_ref.shape[0] // 256
     lefts = l_ref.shape[1] // 32
@@ -198,6 +245,7 @@
     tasks = dl_ref.shape[0] // 32
     groups = tasks // 8
     slots = out_ref.shape[1]
+    half = d_ref.shape[0]
 
     def w_copy(r):
         part = pl.ds(r * aux, aux)
@@ -214,7 +262,11 @@
     own_chunk = iota((256, 128), 0) % 4 == iota((256, 128), 1) // 32
     repeat = ones_where(iota((128, 256), 0) % 32 == iota((128, 256), 1) % 32)
     for g in range(groups):
-        picked = [d_ref[table_ref[g * 8 + u]].astype(F32) for u in range(8)]
+        picked = []
+        for u in range(8):
+            spot = table_ref[g * 8 + u]
+            here = lax.rem(spot, half)
+            picked.append(jnp.where(spot < half, d_ref[here].astype(F32), e_ref[here].astype(F32)))
         e = jnp.dot(spread, jnp.concatenate(picked, axis=0).astype(BF), preferred_element_type=F32)
         e = jnp.where(own_chunk, e, 0.0).astype(BF)
         dl_ref[g * 256:(g + 1) * 256, :] = jnp.dot(e, repeat, preferred_element_type=F32).astype(BF)
@@ -282,13 +334,13 @@
     out_ref[...] = send_ref[...].reshape(out_ref.shape).astype(out_ref.dtype)
 
 
-def run_tasks(table, names, w, l, dens, tasks, peers, cap):
+def run_tasks(table, names, w, l, dens, other, tasks, peers, cap):
     w = pltpu.with_memory_space_constraint(w, pltpu.HBM)
     l = pltpu.with_memory_space_constraint(l, pltpu.HBM)
     return pl.pallas_call(
         tasks_kernel,
         out_shape=jax.ShapeDtypeStruct((peers, cap + 1, 8, 128), BF),
-        in_specs=[SM, VM, HB, HB, VM],
+        in_specs=[SM, VM, HB, HB, VM, VM],
         out_specs=VM,
         scratch_shapes=[
             pltpu.VMEM((tasks * 32, 256), BF),
@@ -301,7 +353,7 @@
             pltpu.SemaphoreType.DMA,
         ],
         compiler_params=pltpu.CompilerParams(vmem_limit_bytes=24 * MB),
-    )(table, names, w, l, dens)
+    )(table, names, w, l, dens, other)
 
 
 def spread_kernel(recv_ref, out_ref, flat_ref):
@@ -371,23 +423,28 @@
 
 def per_device(coeffs, coulomb, density, task_owner, task_slot, task_left, task_right, task_aux, task_dest):
     na = coeffs.shape[1]
-    blk, task = lax.axis_size("blk"), lax.axis_size("task")
+    blk, task = lax.axis_size("x") * lax.axis_size("core"), lax.axis_size("task")
     chips = blk // CORES
-    same_core = [[x * CORES + c for x in range(chips)] for c in range(CORES)]
-    same_chip = [[x * CORES + c for c in range(CORES)] for x in range(chips)]
-    dens = lax.all_to_all(run_pack(density, chips), "blk", 0, 0, tiled=True, axis_index_groups=same_core)
-    me = lax.axis_index("blk").astype(jnp.int32).reshape(1)
-    w, l, table, names = run_prepare(me, task_owner.reshape(-1), task_slot, task_left, task_right, task_aux, task_dest,
-                                     coeffs, coulomb.reshape(coulomb.shape[0] * na, na))
-    dens = lax.all_gather(dens.reshape(chips * HELD, 8, 128), "blk", axis=0, tiled=True, axis_index_groups=same_chip)
-    send = run_tasks(table, names, w, l, dens, task_slot.shape[0], blk, 128 // blk)
-    recv = lax.all_to_all(send, "blk", 0, 0, tiled=True)
+    dens = lax.all_to_all(run_pack(density, chips), "x", 0, 0, tiled=True)
+    me = lax.axis_index(BLK).astype(jnp.int32).reshape(1)
+    l, table, names = run_lefts(me, task_owner.reshape(-1), task_slot, task_left, task_right, task_aux, task_dest, coeffs)
+    dens = dens.reshape(chips * HELD, 8, 128)
+    dens, l, table, names = lax.optimization_barrier((dens, l, table, names))
+    other = lax.ppermute(dens, "core", [(0, 1), (1, 0)])
+    w = run_rights(coeffs, coulomb.reshape(coulomb.shape[0] * na, na), dens)
+    send = run_tasks(table, names, w, l, dens, other, task_slot.shape[0], blk, 128 // blk)
+    recv = lax.all_to_all(send, BLK, 0, 0, tiled=True)
     rows = run_spread(recv, task, BF)
     back = lax.all_to_all(rows, "task", 0, 0, tiled=True)
     return run_final(back).reshape(1, density.shape[1])
 
 
+BLK = ("x", "core")
+
+
 def solution(mesh):
-    every = P(("task", "blk"))
-    placed = (every, every, P("blk"), every, every, every, every, every, every)
-    return jax.shard_map(per_device, mesh=mesh, in_specs=placed, out_specs=every, check_vma=False)
+    sizes = (mesh.shape["task"], mesh.shape["blk"] // CORES, CORES)
+    fine = jax.sharding.Mesh(mesh.devices.reshape(sizes), ("task", "x", "core"))
+    every = P(("task", "x", "core"))
+    placed = (every, every, P(BLK), every, every, every, every, every, every)
+    return jax.shard_map(per_device, mesh=fine, in_specs=placed, out_specs=every, check_vma=False)

time: 115 us -> 90.7 us (0.79)
  starting transfers between devices: 0.01 us -> 17 us
  waiting for transfers between devices: 18.2 us -> 1.4 us
  between operations: 13.5 us -> 0.13 us
  blocking collectives: 53.6 us -> 40.4 us
  Pallas kernels: 26.2 us -> 29.7 us
  local copies, waits for them, and re-layouts: 2.4 us -> 1.17 us
    all_gather x1 -> x0, waiting for transfers between devices: 18.2 us -> none  [per_device(): lax.all_gather(dens.reshape(chips * HELD, 8, 128), 'blk', axis=0, tiled=T...]
    ppermute x0 -> x1, starting transfers between devices: none -> 12.2 us  [per_device(): other = lax.ppermute(dens, 'core', [(0, 1), (1, 0)])]
    all_to_all x2 -> x1, blocking collectives: 21.5 us -> 9.66 us  [per_device(): recv = lax.all_to_all(send, BLK, 0, 0, tiled=True)]
    all_to_all x0 -> x1, starting transfers between devices: none -> 4.84 us  [per_device(): dens = lax.all_to_all(run_pack(density, chips), 'x', 0, 0, tiled=True)]
    pallas_call x1 -> x2, Pallas kernels: 11.5 us -> 14 us  [the longest x1 8.52 us: run_rights(): pl.pallas_call(rights_kernel, out_shape=pltpu.HBM((blocks * aux, tiles *...]
    all_to_all x0 -> x1, waiting for transfers between devices: none -> 1.4 us  [per_device(): dens = lax.all_to_all(run_pack(density, chips), 'x', 0, 0, tiled=True)]
    all_to_all x1, blocking collectives: 32.1 us -> 30.8 us  [per_device(): back = lax.all_to_all(rows, 'task', 0, 0, tiled=True)]
    unnamed x20 -> x18, local copies, waits for them, and re-layouts: 2.28 us -> 1.05 us
  transfers between devices with their start and end apart: 1 -> 2, of which waited for: 1 -> 1; matrix products, arithmetic and copies ran while one was open for 0% -> 0% of each run, Pallas kernels for 10% -> 16%
where the time goes in v3:
time: 90.7 us; the launch traced here: 89.8 us
  blocking collectives  40.4 us (45%)
  Pallas kernels  29.7 us (33%)
  starting transfers between devices  17 us (19%)
  waiting for transfers between devices  1.4 us (2%)
  local copies, waits for them, and re-layouts  1.17 us (1%)
    all_to_all x1, blocking collectives, per_device(): back = lax.all_to_all(rows, 'task', 0, 0, tiled=True)  30.8 us
    pallas_call x1, Pallas kernels, run_tasks(): pl.pallas_call(tasks_kernel, out_shape=jax.ShapeDtypeStruct((peers, cap +...  13.2 us
    ppermute x1, starting transfers between devices, per_device(): other = lax.ppermute(dens, 'core', [(0, 1), (1, 0)])  12.2 us
    all_to_all x1, blocking collectives, per_device(): recv = lax.all_to_all(send, BLK, 0, 0, tiled=True)  9.66 us
    pallas_call x1, Pallas kernels, run_rights(): pl.pallas_call(rights_kernel, out_shape=pltpu.HBM((blocks * aux, tiles *...  8.52 us
    pallas_call x1, Pallas kernels, run_lefts(): pl.pallas_call(lefts_kernel, out_shape=(pltpu.HBM((tiles * 256, blocks *...  5.48 us
    all_to_all x1, starting transfers between devices, per_device(): dens = lax.all_to_all(run_pack(density, chips), 'x', 0, 0, tiled=True)  4.84 us
  transfers between devices with their start and end apart: 2, of which 1 were waited for; matrix products, arithmetic and copies ran while one was open for 0% of the time, Pallas kernels for 16%

profile of v3, /device:TPU:1, one launch (start us, length us, event | category | flops | bytes accessed | tf_op | source)
XLA Modules:
  0.0 89.8 jit_solution(15384285644628491085)
XLA Ops:
  0.0 0.0 copy-start
  0.0 0.0 copy-start.1
  0.0 1.0 %copy-done.1 = bf16[64,1024]{1,0:T(8,128)(2,1)S(1)} copy-done((bf16[64,1024]{1,0:T(8,128)(2,1)S(1)}, bf16[64,1024]{1,0:T(8,128)(2,1)}, u32[]{:S(2)}) %copy-start.1) | copy-done | bytes 131096
  1.0 0.0 copy-start.2
  1.0 0.0 copy-start.3
  1.0 0.0 copy-start.4
  1.0 0.0 copy-start.5
  1.0 0.0 copy-start.6
  1.0 0.0 copy-start.7
  1.1 0.0 copy-start.8
  1.1 1.4 %shard_map.91 = bf16[4,64,8,128]{3,2,1,0:T(8,128)(2,1)} custom-call(bf16[64,1024]{1,0:T(8,128)(2,1)S(1)} %copy-done.1), custom_call_target="tpu_custom_call" | custom-call | tf_op jit(solution)/shard_map/pallas_call | solution.py:47
  2.4 4.8 %all-to-all-start = ((bf16[4,64,8,128]{3,2,1,0:T(8,128)(2,1)}), bf16[4,64,8,128]{3,2,1,0:T(8,128)(2,1)S(1)}, u32[]{:S(2)}, u32[]{:S(2)}) async-start(bf16[4,64,8,128]{3,2,1,0:T(8,128)(2,1)} %shard_map.91), calls=%async_computation | async-start | bytes 1048576 | tf_op jit(solution)/shard_map/all_to_all | solution.py:428
  7.3 0.0 copy-done
  7.3 0.0 copy-done.2
  7.3 0.0 copy-done.3
  7.3 0.0 copy-done.4
  7.3 0.0 copy-done.5
  7.3 0.0 copy-done.6
  7.3 0.0 copy-done.7
  7.3 5.5 %shard_map.92 = (bf16[3072,256]{1,0:T(8,128)(2,1)}, s32[1024]{0:T(1024)S(1)}, f32[8,128]{1,0:T(8,128)S(1)}) custom-call(s32[1]{0:T(128)} %bitcast.1.me_ref, s32[64]{0:T(128)S(1)} %bitcast.7, s32[64]{0:T(128)S(1)} %copy-done.3, s32[64]{0:T(128)S(1)} %copy-done.4, s32[64]{0:T(128)S(1)} %copy-done.5, s32[64]{0:T(128)S(1)} %copy-done.6, s32[64]{0:T(128)S(1)} %copy-done.7, ...), custom_call_target="tpu_custom_call" | custom-call | tf_op jit(solution)/shard_map/pallas_call | solution.py:156
  12.8 1.4 %all-to-all-done = bf16[4,64,8,128]{3,2,1,0:T(8,128)(2,1)S(1)} async-done(((bf16[4,64,8,128]{3,2,1,0:T(8,128)(2,1)}), bf16[4,64,8,128]{3,2,1,0:T(8,128)(2,1)S(1)}, u32[]{:S(2)}, u32[]{:S(2)}) %all-to-all-start) | async-done | bytes 524320 | tf_op jit(solution)/shard_map/all_to_all | solution.py:428
  14.2 12.2 %collective-permute-start = (bf16[256,8,128]{2,1,0:T(8,128)(2,1)S(1)}, bf16[256,8,128]{2,1,0:T(8,128)(2,1)S(1)}, u32[]{:S(2)}, u32[]{:S(2)}) collective-permute-start(bf16[256,8,128]{2,1,0:T(8,128)(2,1)S(1)} %bitcast.4), channel_id=1, source_target_pairs={{0,1},{1,0},{2,3},{3,2},{4,5},{5,4},{6,7},{7,6},{8,9},{9,8},{10,11... | collective-permute-start | bytes 1572872 | tf_op jit(solution)/shard_map/ppermute | solution.py:433
  26.4 0.0 copy-done.8
  26.4 0.1 reshape.18.coulomb_ref
  26.5 8.5 %shard_map.93.w_in = bf16[32,384,256]{2,1,0:T(8,128)(2,1)} custom-call(bf16[8,96,1024]{2,1,0:T(8,128)(2,1)S(1)} %copy-done, bf16[384,96]{1,0:T(8,128)(2,1)S(1)} %reshape.18.coulomb_ref, bf16[256,8,128]{2,1,0:T(8,128)(2,1)S(1)} %bitcast.5), custom_call_target="tpu_custom_call" | custom-call | tf_op jit(solution)/shard_map/pallas_call | solution.py:222
  35.0 0.0 collective-permute-done.e_ref
  35.0 13.2 %shard_map.94 = bf16[8,17,8,128]{3,2,1,0:T(8,128)(2,1)S(1)} custom-call(s32[1024]{0:T(1024)S(1)} %get-tuple-element.15.table_ref, f32[8,128]{1,0:T(8,128)S(1)} %get-tuple-element.16.names_ref, bf16[32,384,256]{2,1,0:T(8,128)(2,1)} %shard_map.93.w_in, bf16[3072,256]{1,0:T(8,128)(2,1)} %get-tuple-element.18.l_in, bf16[256,8,128]{2,1,0:T(8,128)(2,1)S(1)} %bitcast.6, ...), custom_call_target="tpu_custom_call" | custom-call | tf_op jit(solution)/shard_map/pallas_call | solution.py:340
  48.3 9.7 %all_to_all.15.recv_ref = bf16[8,17,8,128]{3,2,1,0:T(8,128)(2,1)S(1)} all-to-all(bf16[8,17,8,128]{3,2,1,0:T(8,128)(2,1)S(1)} %shard_map.94), channel_id=1, replica_groups=mesh['task'=96,'x'=4,'core'=2] {'x','core'}, dimensions={0} | all-to-all | bytes 557056 | tf_op jit(solution)/shard_map/all_to_all | solution.py:436
  57.9 0.3 shard_map.95
  58.2 30.8 %all_to_all.16.recv_ref = bf16[96,8,128]{2,1,0:T(8,128)(2,1)S(1)} all-to-all(bf16[96,8,128]{2,1,0:T(8,128)(2,1)S(1)} %shard_map.95), channel_id=1, replica_groups=mesh['task'=96,'x'=4,'core'=2] {'task'}, dimensions={0} | all-to-all | bytes 393216 | tf_op jit(solution)/shard_map/all_to_all | solution.py:438
  89.0 0.9 shard_map.96
Async XLA Ops:
  0.0 7.3 %copy-start = (bf16[8,96,1024]{2,1,0:T(8,128)(2,1)S(1)}, bf16[8,96,1024]{2,1,0:T(8,128)(2,1)}, u32[]{:S(2)}) copy-start(bf16[8,96,1024]{2,1,0:T(8,128)(2,1)} %coeffs_ref.3) | copy-start | bytes 4718596
  0.0 1.0 %copy-start.1 = (bf16[64,1024]{1,0:T(8,128)(2,1)S(1)}, bf16[64,1024]{1,0:T(8,128)(2,1)}, u32[]{:S(2)}) copy-start(bf16[64,1024]{1,0:T(8,128)(2,1)} %d_ref.1) | copy-start | bytes 393220
  1.0 6.2 %copy-start.2 = (s32[64,1]{0,1:T(1,128)S(1)}, s32[64,1]{0,1:T(1,128)}, u32[]{:S(2)}) copy-start(s32[64,1]{0,1:T(1,128)} %param.12) | copy-start | bytes 772
  1.0 6.2 %copy-start.3 = (s32[64]{0:T(128)S(1)}, s32[64]{0:T(128)}, u32[]{:S(2)}) copy-start(s32[64]{0:T(128)} %slot_ref.1) | copy-start | bytes 772
  1.0 6.2 %copy-start.4 = (s32[64]{0:T(128)S(1)}, s32[64]{0:T(128)}, u32[]{:S(2)}) copy-start(s32[64]{0:T(128)} %left_ref.1) | copy-start | bytes 772
  1.0 6.3 %copy-start.5 = (s32[64]{0:T(128)S(1)}, s32[64]{0:T(128)}, u32[]{:S(2)}) copy-start(s32[64]{0:T(128)} %right_ref.1) | copy-start | bytes 772
  1.0 6.3 %copy-start.6 = (s32[64]{0:T(128)S(1)}, s32[64]{0:T(128)}, u32[]{:S(2)}) copy-start(s32[64]{0:T(128)} %aux_ref.1) | copy-start | bytes 772
  1.0 6.3 %copy-start.7 = (s32[64]{0:T(128)S(1)}, s32[64]{0:T(128)}, u32[]{:S(2)}) copy-start(s32[64]{0:T(128)} %dest_ref.1) | copy-start | bytes 772
  1.1 25.3 %copy-start.8 = (bf16[4,9216]{1,0:T(4,128)(2,1)S(1)}, bf16[4,9216]{1,0:T(4,128)(2,1)}, u32[]{:S(2)}) copy-start(bf16[4,9216]{1,0:T(4,128)(2,1)} %param.10) | copy-start | bytes 221188
  2.4 11.8 %all-to-all-start = ((bf16[4,64,8,128]{3,2,1,0:T(8,128)(2,1)}), bf16[4,64,8,128]{3,2,1,0:T(8,128)(2,1)S(1)}, u32[]{:S(2)}, u32[]{:S(2)}) async-start(bf16[4,64,8,128]{3,2,1,0:T(8,128)(2,1)} %shard_map.91), calls=%async_computation | async-start | bytes 1048576 | tf_op jit(solution)/shard_map/all_to_all | solution.py:428
  14.2 20.8 %collective-permute-start = (bf16[256,8,128]{2,1,0:T(8,128)(2,1)S(1)}, bf16[256,8,128]{2,1,0:T(8,128)(2,1)S(1)}, u32[]{:S(2)}, u32[]{:S(2)}) collective-permute-start(bf16[256,8,128]{2,1,0:T(8,128)(2,1)S(1)} %bitcast.4), channel_id=1, source_target_pairs={{0,1},{1,0},{2,3},{3,2},{4,5},{5,4},{6,7},{7,6},{8,9},{9,8},{10,11... | collective-permute-start | bytes 1572872 | tf_op jit(solution)/shard_map/ppermute | solution.py:433

commit v4 on v3

v4 whole, which is shorter than its diff:
```python
import functools

import jax
import jax.numpy as jnp
from jax import lax
from jax.experimental import pallas as pl
from jax.experimental.pallas import tpu as pltpu
from jax.sharding import PartitionSpec as P

BF = jnp.bfloat16
F32 = jnp.float32
MB = 2**20
VM = pl.BlockSpec(memory_space=pltpu.VMEM)
SM = pl.BlockSpec(memory_space=pltpu.SMEM)
HB = pl.BlockSpec(memory_space=pltpu.HBM)
PEERS = 8
CORES = 2
HELD = 64
AUX = 4
CUT1, CUT2 = 3, 6


def iota(shape, dim):
    return lax.broadcasted_iota(jnp.int32, shape, dim)


def ones_where(mask):
    return jnp.where(mask, 1.0, 0.0).astype(BF)


def pack_kernel(d_ref, out_ref, flat_ref):
    blocks, cells = d_ref.shape
    d = d_ref[...]
    for b in range(cells // 256):
        col = iota((1, 256), 1) + b * 256
        source = ((col & 31) << 5) + (col >> 5)
        y = jnp.zeros((blocks, 256), F32)
        for a in range(cells // 256):
            move = ones_where(iota((256, 256), 0) == source - a * 256)
            y += jnp.dot(d[:, a * 256:(a + 1) * 256], move, preferred_element_type=F32)
        for e in range(2):
            flat_ref[pl.ds(2 * b + e, blocks, stride=8), :] = y[:, e * 128:(e + 1) * 128]
    x = flat_ref[...].reshape(blocks, 8, 128).astype(BF)
    for p in range(out_ref.shape[0]):
        out_ref[p] = x


def run_pack(density, peers):
    blocks = density.shape[0]
    return pl.pallas_call(
        pack_kernel,
        out_shape=jax.ShapeDtypeStruct((peers, blocks, 8, 128), BF),
        in_specs=[VM],
        out_specs=VM,
        scratch_shapes=[pltpu.VMEM((blocks * 8, 128), F32)],
        compiler_params=pltpu.CompilerParams(vmem_limit_bytes=8 * MB),
    )(density)


def lane_move():
    col = iota((1, 512), 1)
    source = ((col & 96) << 2) + ((col >> 7) << 5) + (col & 31)
    return ones_where(iota((512, 512), 0) == source)


def put_rows(y_ref, full, q, count):
    for e in range(2):
        v = 2 * q + e
        for mt in range(count):
            y_ref[mt * 64 + v * 8:mt * 64 + v * 8 + 8, :] = full[mt * 8:mt * 8 + 8, e * 128:(e + 1) * 128]


def gather_rows(y_ref, x_ref, first, count):
    for mt in range(first, first + count):
        for m in range(4):
            pair = [y_ref[pl.ds(mt * 64 + 4 * h + m, 8, stride=8), :] for h in range(2)]
            x_ref[mt * 16:(mt + 1) * 16, m * 128:(m + 1) * 128] = jnp.concatenate(pair, axis=0).astype(BF)


def turned(x_ref, move_ref, first, tiles):
    z = jnp.dot(x_ref[first * 16:(first + tiles) * 16, :], move_ref[...], preferred_element_type=F32)
    blocks = []
    for s in range(tiles):
        halves = []
        for h in range(2):
            row = (s * 2 + h) * 8
            halves.append(jnp.concatenate([z[row:row + 8, c * 128:(c + 1) * 128] for c in range(4)], axis=0))
        blocks.append(jnp.concatenate(halves, axis=1).astype(BF))
    return blocks


def lefts_kernel(me_ref, owner_ref, slot_ref, left_ref, right_ref, aux_ref, dest_ref, coeffs_ref,
                 l_out, table_ref, names_ref, count_ref, y0_ref, y1_ref, x0_ref, x1_ref, move_ref, lw_ref, l_ref, l_sem):
    blocks, na, cells = coeffs_ref.shape
    tiles = na // 8
    tasks = slot_ref.shape[0]
    share = tasks // blocks
    peers, cap = PEERS, 128 // PEERS
    sub, lane = iota((8, 128), 0), iota((8, 128), 1)
    me = me_ref[0]
    for b in range(peers):
        count_ref[b] = 0
    move_ref[...] = lane_move()

    def place_some(r, names):
        for u in range(share):
            t = r * share + u
            dest = dest_ref[t]
            peer = lax.rem(dest, peers)
            place = count_ref[peer]
            count_ref[peer] = place + 1
            owner = owner_ref[t]
            table_ref[t] = lax.rem(owner + me, CORES) * (HELD * peers // CORES) + owner // CORES * HELD + slot_ref[t]
            table_ref[tasks + t] = right_ref[t] * AUX + aux_ref[t]
            table_ref[2 * tasks + t] = left_ref[t]
            table_ref[3 * tasks + t] = peer * (cap + 1) + place
            name = (dest // peers + 1).astype(F32)
            names = jnp.where((sub == peer) & (lane == me * cap + place), name, names)
        return names

    def two(h, names):
        for e, (y_ref, x_ref) in enumerate(((y0_ref, x0_ref), (y1_ref, x1_ref))):
            r = 2 * h + e
            for q in range(cells // 256):
                put_rows(y_ref, coeffs_ref[r, :, q * 256:(q + 1) * 256].astype(F32), q, tiles)
            gather_rows(y_ref, x_ref, 0, tiles)
            for s, block in enumerate(turned(x_ref, move_ref, 0, tiles)):
                lw_ref[s, pl.ds(pl.multiple_of(r * 32, 32), 32), :] = block
            names = place_some(r, names)
        return names

    names_ref[...] = lax.fori_loop(0, blocks // 2, two, jnp.zeros((8, 128), F32), unroll=4)
    copies = []
    for s in range(tiles):
        part = pl.ds(s * 256, 256)
        l_ref[part, :] = jnp.transpose(lw_ref[s])
        copies.append(pltpu.make_async_copy(l_ref.at[part], l_out.at[part], l_sem.at[s]))
        copies[s].start()
    for copy in copies:
        copy.wait()


def run_lefts(me, owner, slot, left, right, aux_of, dest, coeffs):
    blocks, na, cells = coeffs.shape
    tiles = na // 8
    return pl.pallas_call(
        lefts_kernel,
        out_shape=(
            pltpu.HBM((tiles * 256, blocks * 32), BF),
            jax.ShapeDtypeStruct((1024,), jnp.int32),
            jax.ShapeDtypeStruct((8, 128), F32),
        ),
        in_specs=[SM] * 7 + [VM],
        out_specs=(HB, SM, VM),
        scratch_shapes=[
            pltpu.SMEM((PEERS,), jnp.int32),
            pltpu.VMEM((na * 8, 128), F32),
            pltpu.VMEM((na * 8, 128), F32),
            pltpu.VMEM((na * 2, 512), BF),
            pltpu.VMEM((na * 2, 512), BF),
            pltpu.VMEM((512, 512), BF),
            pltpu.VMEM((tiles, blocks * 32, 256), BF),
            pltpu.VMEM((tiles * 256, blocks * 32), BF),
            pltpu.SemaphoreType.DMA((tiles,)),
        ],
        compiler_params=pltpu.CompilerParams(vmem_limit_bytes=16 * MB),
    )(me, owner, slot, left, right, aux_of, dest, coeffs)


def multiply(coeffs_ref, coulomb_ref, r, y_ref):
    cells = coeffs_ref.shape[2]
    count = coulomb_ref.shape[0] // 8
    for q in range(cells // 256):
        y = jnp.dot(coulomb_ref[...], coeffs_ref[r, :, q * 256:(q + 1) * 256], preferred_element_type=F32)
        put_rows(y_ref, y, q, count)


def turn(y_ref, x_ref, move_ref, w_ref, first, tiles):
    for a in range(y_ref.shape[0] // (64 * tiles)):
        gather_rows(y_ref, x_ref, a * tiles, tiles)
        for s, block in enumerate(turned(x_ref, move_ref, a * tiles, tiles)):
            w_ref[first + a, s * 32:(s + 1) * 32, :] = block


def rights_kernel(begin, end, coeffs_ref, coulomb_ref, after_ref, w_out, y0_ref, y1_ref, x0_ref, x1_ref, move_ref, w_ref, w_sem):
    na = coeffs_ref.shape[1]
    aux = coulomb_ref.shape[0] // na
    tiles = na // 8
    move_ref[...] = lane_move()
    ys, xs = (y0_ref, y1_ref), (x0_ref, x1_ref)
    copies = []
    multiply(coeffs_ref, coulomb_ref, begin, ys[0])
    for r in range(begin, end):
        e = (r - begin) % 2
        if r + 1 < end:
            multiply(coeffs_ref, coulomb_ref, r + 1, ys[1 - e])
        turn(ys[e], xs[e], move_ref, w_ref, (r - begin) * aux, tiles)
        part = pl.ds((r - begin) * aux, aux)
        copies.append(pltpu.make_async_copy(w_ref.at[part], w_out.at[part], w_sem.at[r - begin]))
        copies[-1].start()
    for copy in copies:
        copy.wait()


def rights_scratch(rows):
    return [
        pltpu.VMEM((rows * 8, 128), F32),
        pltpu.VMEM((rows * 8, 128), F32),
        pltpu.VMEM((rows * 2, 512), BF),
        pltpu.VMEM((rows * 2, 512), BF),
        pltpu.VMEM((512, 512), BF),
    ]


def run_rights(coeffs, vall, after, begin, end):
    na = coeffs.shape[1]
    aux = vall.shape[0] // na
    shape = ((end - begin) * aux, na // 8 * 32, 256)
    return pl.pallas_call(
        functools.partial(rights_kernel, begin, end),
        out_shape=pltpu.HBM(shape, BF),
        in_specs=[VM, VM, pl.BlockSpec(memory_space=pl.ANY)],
        out_specs=HB,
        scratch_shapes=rights_scratch(vall.shape[0]) + [
            pltpu.VMEM(shape, BF),
            pltpu.SemaphoreType.DMA((end - begin,)),
        ],
        compiler_params=pltpu.CompilerParams(vmem_limit_bytes=20 * MB),
    )(coeffs, vall, after)


def tasks_kernel(table_ref, names_ref, coeffs_ref, coulomb_ref, w1_in, w2_in, l_in, d_ref, e_ref,
                 out_ref, y0_ref, y1_ref, x0_ref, x1_ref, move_ref, dl_ref, a_ref, send_ref, w_ref, l_ref, sem):
    tiles = l_ref.shape[0] // 256
    blocks = l_ref.shape[1] // 32
    aux = w_ref.shape[0] // blocks
    tasks = dl_ref.shape[0] // 32
    groups = tasks // 8
    slots = out_ref.shape[1]
    half = d_ref.shape[0]

    here = pl.ds(0, w1_in.shape[0])
    there = pl.ds(w1_in.shape[0], w2_in.shape[0])
    copies = [
        pltpu.make_async_copy(l_in, l_ref, sem.at[0]),
        pltpu.make_async_copy(w1_in, w_ref.at[here], sem.at[1]),
        pltpu.make_async_copy(w2_in, w_ref.at[there], sem.at[2]),
    ]
    for i in (1, 2, 0):
        copies[i].start()
    move_ref[...] = lane_move()
    ys, xs = (y0_ref, y1_ref), (x0_ref, x1_ref)
    begin = (w1_in.shape[0] + w2_in.shape[0]) // aux
    for r in range(begin, blocks):
        multiply(coeffs_ref, coulomb_ref, r, ys[r % 2])
    for r in range(begin, blocks):
        turn(ys[r % 2], xs[r % 2], move_ref, w_ref, r * aux, tiles)
    send_ref[...] = jnp.zeros_like(send_ref)

    spread = ones_where((iota((256, 64), 0) >> 2) == iota((256, 64), 1))
    own_chunk = (iota((256, 128), 0) & 3) == (iota((256, 128), 1) >> 5)
    repeat = ones_where((iota((128, 256), 0) & 31) == (iota((128, 256), 1) & 31))
    for g in range(groups):
        picked = []
        for u in range(8):
            spot = table_ref[g * 8 + u]
            here = lax.rem(spot, half)
            picked.append(jnp.where(spot < half, d_ref[here].astype(F32), e_ref[here].astype(F32)))
        e = jnp.dot(spread, jnp.concatenate(picked, axis=0).astype(BF), preferred_element_type=F32)
        e = jnp.where(own_chunk, e, 0.0).astype(BF)
        dl_ref[g * 256:(g + 1) * 256, :] = jnp.dot(e, repeat, preferred_element_type=F32).astype(BF)

    diag = ones_where((iota((256, 256), 0) >> 5) == (iota((256, 256), 1) >> 5))
    fold = ones_where((iota((256, 128), 0) & 31) == (iota((256, 128), 1) & 31))
    chunk = iota((8, 128), 1) >> 5
    column = iota((32, 256), 1) >> 5

    def apply(g, carry):
        for u in range(64):
            t = g * 64 + u
            rows = pl.ds(pl.multiple_of(t * 32, 32), 32)
            bd = jnp.concatenate([dl_ref[rows, :]] * 8, axis=0) * diag
            y = jnp.dot(w_ref[table_ref[tasks + t]], bd, preferred_element_type=F32).astype(BF)
            for s in range(tiles):
                a_ref[rows, s * 256:(s + 1) * 256] = y[s * 32:(s + 1) * 32, :]
        return carry

    def close(g, carry):
        rows = pl.ds(pl.multiple_of(g * 2048, 2048), 2048)
        total = jnp.dot(a_ref[rows, :], l_ref[...], preferred_element_type=F32)
        own = [jnp.where(column == table_ref[2 * tasks + g * 64 + u], total[u * 32:(u + 1) * 32, :], 0.0) for u in range(64)]
        total = jnp.dot(jnp.concatenate(own, axis=0).astype(BF), fold, preferred_element_type=F32)
        for u in range(64):
            block = total[u * 32:u * 32 + 8, :]
            for q in range(1, 4):
                block = jnp.where(chunk == q, total[u * 32 + q * 8:u * 32 + q * 8 + 8, :], block)
            send_ref[table_ref[3 * tasks + g * 64 + u]] = block
        return carry

    copies[1].wait()
    copies[2].wait()
    lax.fori_loop(0, tasks // 64, apply, 0)
    copies[0].wait()
    lax.fori_loop(0, tasks // 64, close, 0)
    names = names_ref[...]
    for p in range(out_ref.shape[0]):
        send_ref[p * slots + slots - 1] = jnp.broadcast_to(names[p:p + 1, :], (8, 128))
    out_ref[...] = send_ref[...].reshape(out_ref.shape).astype(out_ref.dtype)


def run_tasks(table, names, coeffs, vall, w1, w2, l, dens, other, tasks, peers, cap):
    w1, w2, l = (pltpu.with_memory_space_constraint(x, pltpu.HBM) for x in (w1, w2, l))
    blocks, na, _ = coeffs.shape
    return pl.pallas_call(
        tasks_kernel,
        out_shape=jax.ShapeDtypeStruct((peers, cap + 1, 8, 128), BF),
        in_specs=[SM, VM, VM, VM, HB, HB, HB, VM, VM],
        out_specs=VM,
        scratch_shapes=rights_scratch(vall.shape[0]) + [
            pltpu.VMEM((tasks * 32, 256), BF),
            pltpu.VMEM((tasks * 32, l.shape[0]), BF),
            pltpu.VMEM((peers * (cap + 1), 8, 128), F32),
            pltpu.VMEM((blocks * (vall.shape[0] // na),) + w1.shape[1:], BF),
            pltpu.VMEM(l.shape, BF),
            pltpu.SemaphoreType.DMA((3,)),
        ],
        compiler_params=pltpu.CompilerParams(vmem_limit_bytes=40 * MB),
    )(table, names, coeffs, vall, w1, w2, l, dens, other)


def spread_kernel(recv_ref, out_ref, flat_ref):
    peers, slots = recv_ref.shape[0], recv_ref.shape[1]
    cap = slots - 1
    rows = out_ref.shape[0]
    names = recv_ref[0, cap].astype(F32)
    for p in range(1, peers):
        names = names + recv_ref[p, cap].astype(F32)
    names = jnp.broadcast_to(names[0:1, :], (rows, 128)).astype(jnp.int32)
    hot = ones_where(iota((rows, 128), 0) + 1 == names)
    for p in range(peers):
        for n in range(cap):
            flat_ref[(p * cap + n) * 8:(p * cap + n + 1) * 8, :] = recv_ref[p, n].astype(F32)
    sums = []
    for i in range(8):
        x = flat_ref[pl.ds(i, 128, stride=8), :]
        sums.append(jnp.dot(hot, x.astype(BF), preferred_element_type=F32))
    for i in range(8):
        flat_ref[pl.ds(i, rows, stride=8), :] = sums[i]
    out_ref[...] = flat_ref[0:rows * 8, :].reshape(rows, 8, 128).astype(out_ref.dtype)


def run_spread(recv, rows, dtype):
    peers, slots = recv.shape[:2]
    return pl.pallas_call(
        spread_kernel,
        out_shape=jax.ShapeDtypeStruct((rows, 8, 128), dtype),
        in_specs=[VM],
        out_specs=VM,
        scratch_shapes=[pltpu.VMEM((max(rows, peers * (slots - 1)) * 8, 128), F32)],
        compiler_params=pltpu.CompilerParams(vmem_limit_bytes=8 * MB),
    )(recv)


def exact_dot(x, y):
    out = None
    for _ in range(3):
        part = x.astype(BF)
        x = x - part.astype(F32)
        term = jnp.dot(part, y, preferred_element_type=F32)
        out = term if out is None else out + term
    return out


def final_kernel(recv_ref, out_ref):
    total = jnp.sum(recv_ref[...].astype(F32), axis=0) * -0.25
    vi = iota((64, 128), 0) >> 3
    wide = jnp.concatenate([total] * 8, axis=0)
    wide = jnp.where((iota((64, 128), 1) & 7) == vi, wide, 0.0)
    r, c = iota((128, 128), 0), iota((128, 128), 1)
    move = ones_where((r >> 3) == ((c & 3) << 2) + (c >> 5))
    wide = exact_dot(wide, move)
    wide = jnp.where(((iota((64, 128), 1) >> 2) & 7) == (iota((64, 128), 0) & 7), wide, 0.0)
    out_ref[...] = jnp.sum(wide.reshape(8, 8, 128), axis=1)


def run_final(recv):
    return pl.pallas_call(
        final_kernel,
        out_shape=jax.ShapeDtypeStruct((8, 128), F32),
        in_specs=[VM],
        out_specs=VM,
        compiler_params=pltpu.CompilerParams(vmem_limit_bytes=4 * MB),
    )(recv)


def per_device(coeffs, coulomb, density, task_owner, task_slot, task_left, task_right, task_aux, task_dest):
    na = coeffs.shape[1]
    blk, task = lax.axis_size("x") * lax.axis_size("core"), lax.axis_size("task")
    chips = blk // CORES
    dens = lax.all_to_all(run_pack(density, chips), "x", 0, 0, tiled=True)
    me = lax.axis_index(BLK).astype(jnp.int32).reshape(1)
    vall = coulomb.reshape(coulomb.shape[0] * na, na)
    l, table, names = run_lefts(me, task_owner.reshape(-1), task_slot, task_left, task_right, task_aux, task_dest, coeffs)
    w1 = run_rights(coeffs, vall, names, 0, CUT1)
    dens = dens.reshape(chips * HELD, 8, 128)
    dens, l, table, names, w1 = lax.optimization_barrier((dens, l, table, names, w1))
    other = lax.ppermute(dens, "core", [(0, 1), (1, 0)])
    w2 = run_rights(coeffs, vall, dens, CUT1, CUT2)
    send = run_tasks(table, names, coeffs, vall, w1, w2, l, dens, other, task_slot.shape[0], blk, 128 // blk)
    recv = lax.all_to_all(send, BLK, 0, 0, tiled=True)
    rows = run_spread(recv, task, BF)
    back = lax.all_to_all(rows, "task", 0, 0, tiled=True)
    return run_final(back).reshape(1, density.shape[1])


BLK = ("x", "core")


def solution(mesh):
    sizes = (mesh.shape["task"], mesh.shape["blk"] // CORES, CORES)
    fine = jax.sharding.Mesh(mesh.devices.reshape(sizes), ("task", "x", "core"))
    every = P(("task", "x", "core"))
    placed = (every, every, P(BLK), every, every, every, every, every, every)
    return jax.shard_map(per_device, mesh=fine, in_specs=placed, out_specs=every, check_vma=False)
```

time: 90.7 us -> 88.9 us (0.980)
  Pallas kernels: 29.7 us -> 24.5 us
  local copies, waits for them, and re-layouts: 1.17 us -> 5.96 us
  waiting for transfers between devices: 1.4 us -> 0.01 us
    unnamed x18 -> x16, local copies, waits for them, and re-layouts: 1.05 us -> 4.95 us
    all_to_all x1, blocking collectives: 9.66 us -> 11.9 us  [per_device(): recv = lax.all_to_all(send, BLK, 0, 0, tiled=True)]
    pallas_call x1, Pallas kernels: 13.2 us -> 11.1 us  [run_tasks(): pl.pallas_call(tasks_kernel, out_shape=jax.ShapeDtypeStruct((peers, cap +...]
    pallas_call x1 -> x2, Pallas kernels: 8.52 us -> 6.81 us  [run_rights(): pl.pallas_call(functools.partial(rights_kernel, begin, end), out_shape=pl...]
    all_to_all x1, waiting for transfers between devices: 1.4 us -> 0.01 us  [per_device(): dens = lax.all_to_all(run_pack(density, chips), 'x', 0, 0, tiled=True)]
    pallas_call x1, Pallas kernels: 5.48 us -> 4.1 us  [run_lefts(): pl.pallas_call(lefts_kernel, out_shape=(pltpu.HBM((tiles * 256, blocks *...]
    all_to_all x1, blocking collectives: 30.8 us -> 29.4 us  [per_device(): back = lax.all_to_all(rows, 'task', 0, 0, tiled=True)]
    ppermute x1, starting transfers between devices: 12.2 us -> 11.2 us  [per_device(): other = lax.ppermute(dens, 'core', [(0, 1), (1, 0)])]
  transfers between devices with their start and end apart: 2 -> 2, of which waited for: 1 -> 0; matrix products, arithmetic and copies ran while one was open for 0% -> 1% of each run, Pallas kernels for 16% -> 12%
where the time goes in v4:
time: 88.9 us; the launch traced here: 88 us
  blocking collectives  41.3 us (46%)
  Pallas kernels  24.5 us (28%)
  starting transfers between devices  16.1 us (18%)
  local copies, waits for them, and re-layouts  5.96 us (7%)
    all_to_all x1, blocking collectives, per_device(): back = lax.all_to_all(rows, 'task', 0, 0, tiled=True)  29.4 us
    all_to_all x1, blocking collectives, per_device(): recv = lax.all_to_all(send, BLK, 0, 0, tiled=True)  11.9 us
    ppermute x1, starting transfers between devices, per_device(): other = lax.ppermute(dens, 'core', [(0, 1), (1, 0)])  11.2 us
    pallas_call x1, Pallas kernels, run_tasks(): pl.pallas_call(tasks_kernel, out_shape=jax.ShapeDtypeStruct((peers, cap +...  11.1 us
    pallas_call x2, Pallas kernels, run_rights(): pl.pallas_call(functools.partial(rights_kernel, begin, end), out_shape=pl...  6.81 us
    unnamed x16, local copies, waits for them, and re-layouts  4.95 us
    all_to_all x1, starting transfers between devices, per_device(): dens = lax.all_to_all(run_pack(density, chips), 'x', 0, 0, tiled=True)  4.84 us
    pallas_call x1, Pallas kernels, run_lefts(): pl.pallas_call(lefts_kernel, out_shape=(pltpu.HBM((tiles * 256, blocks *...  4.1 us
  transfers between devices with their start and end apart: 2, of which 0 were waited for; matrix products, arithmetic and copies ran while one was open for 1% of the time, Pallas kernels for 12%

profile of v4, /device:TPU:1, one launch (start us, length us, event | category | flops | bytes accessed | tf_op | source)
XLA Modules:
  0.0 88.0 jit_solution(15170284107462222551)
XLA Ops:
  0.0 0.0 copy-start
  0.0 0.0 copy-start.1
  0.0 1.0 %copy-done.1 = bf16[64,1024]{1,0:T(8,128)(2,1)S(1)} copy-done((bf16[64,1024]{1,0:T(8,128)(2,1)S(1)}, bf16[64,1024]{1,0:T(8,128)(2,1)}, u32[]{:S(2)}) %copy-start.1) | copy-done | bytes 131096
  1.0 1.3 %shard_map.91 = bf16[4,64,8,128]{3,2,1,0:T(8,128)(2,1)} custom-call(bf16[64,1024]{1,0:T(8,128)(2,1)S(1)} %copy-done.1), custom_call_target="tpu_custom_call" | custom-call | tf_op jit(solution)/shard_map/pallas_call | solution.py:50
  2.4 4.8 %all-to-all-start = ((bf16[4,64,8,128]{3,2,1,0:T(8,128)(2,1)}), bf16[4,64,8,128]{3,2,1,0:T(8,128)(2,1)S(1)}, u32[]{:S(2)}, u32[]{:S(2)}) async-start(bf16[4,64,8,128]{3,2,1,0:T(8,128)(2,1)} %shard_map.91), calls=%async_computation | async-start | bytes 1048576 | tf_op jit(solution)/shard_map/all_to_all | solution.py:400
  7.2 1.0 %reshape.18.coulomb_ref = bf16[384,96]{1,0:T(8,128)(2,1)S(1)} reshape(bf16[4,9216]{1,0:T(4,128)(2,1)} %param.10) | data formatting | bytes 147456 | tf_op jit(solution)/shard_map/reshape | solution.py:402
  8.2 0.0 copy-done
  8.3 0.0 copy-start.2
  8.3 0.6 copy-done.2
  8.9 0.0 copy-start.3
  8.9 0.7 copy-done.3
  9.6 0.0 copy-start.4
  9.6 0.7 copy-done.4
  10.2 0.0 copy-start.5
  10.2 0.7 copy-done.5
  10.9 0.0 copy-start.6
  10.9 0.7 copy-done.6
  11.5 0.0 copy-start.7
  11.5 0.7 copy-done.7
  12.2 4.1 %shard_map.92 = (bf16[3072,256]{1,0:T(8,128)(2,1)}, s32[1024]{0:T(1024)S(1)}, f32[8,128]{1,0:T(8,128)S(1)}) custom-call(s32[1]{0:T(128)} %bitcast.1.me_ref, s32[64]{0:T(128)S(1)} %bitcast.7, s32[64]{0:T(128)S(1)} %copy-done.3, s32[64]{0:T(128)S(1)} %copy-done.4, s32[64]{0:T(128)S(1)} %copy-done.5, s32[64]{0:T(128)S(1)} %copy-done.6, s32[64]{0:T(128)S(1)} %copy-done.7, ...), custom_call_target="tpu_custom_call" | custom-call | tf_op jit(solution)/shard_map/pallas_call | solution.py:146
  16.3 3.4 %shard_map.93.w1_in = bf16[12,384,256]{2,1,0:T(8,128)(2,1)} custom-call(bf16[8,96,1024]{2,1,0:T(8,128)(2,1)S(1)} %copy-done, bf16[384,96]{1,0:T(8,128)(2,1)S(1)} %reshape.18.coulomb_ref, f32[8,128]{1,0:T(8,128)S(1)} %get-tuple-element.17.after_ref.names_ref), custom_call_target="tpu_custom_call" | custom-call | tf_op jit(solution)/shard_map/pallas_call | solution.py:219
  19.7 0.0 all-to-all-done
  19.7 11.2 %collective-permute-start = (bf16[256,8,128]{2,1,0:T(8,128)(2,1)S(1)}, bf16[256,8,128]{2,1,0:T(8,128)(2,1)S(1)}, u32[]{:S(2)}, u32[]{:S(2)}) collective-permute-start(bf16[256,8,128]{2,1,0:T(8,128)(2,1)S(1)} %bitcast.4), channel_id=1, source_target_pairs={{0,1},{1,0},{2,3},{3,2},{4,5},{5,4},{6,7},{7,6},{8,9},{9,8},{10,11... | collective-permute-start | bytes 1572872 | tf_op jit(solution)/shard_map/ppermute | solution.py:407
  31.0 3.4 %shard_map.94.w2_in = bf16[12,384,256]{2,1,0:T(8,128)(2,1)} custom-call(bf16[8,96,1024]{2,1,0:T(8,128)(2,1)S(1)} %copy-done, bf16[384,96]{1,0:T(8,128)(2,1)S(1)} %reshape.18.coulomb_ref, bf16[256,8,128]{2,1,0:T(8,128)(2,1)S(1)} %bitcast.5), custom_call_target="tpu_custom_call" | custom-call | tf_op jit(solution)/shard_map/pallas_call | solution.py:219
  34.4 0.0 collective-permute-done.e_ref
  34.4 11.1 %shard_map.95 = bf16[8,17,8,128]{3,2,1,0:T(8,128)(2,1)S(1)} custom-call(s32[1024]{0:T(1024)S(1)} %get-tuple-element.16.table_ref, f32[8,128]{1,0:T(8,128)S(1)} %get-tuple-element.17.after_ref.names_ref, bf16[8,96,1024]{2,1,0:T(8,128)(2,1)S(1)} %copy-done, bf16[384,96]{1,0:T(8,128)(2,1)S(1)} %reshape.18.coulomb_ref, bf16[12,384,256]{2,1,0:T(8,128)(2,1)} %shard_map.93.w1_in, ...), custom_call_target="tpu_custom_call" | custom-call | tf_op jit(solution)/shard_map/pallas_call | solution.py:314
  45.5 11.9 %all_to_all.15.recv_ref = bf16[8,17,8,128]{3,2,1,0:T(8,128)(2,1)S(1)} all-to-all(bf16[8,17,8,128]{3,2,1,0:T(8,128)(2,1)S(1)} %shard_map.95), channel_id=1, replica_groups=mesh['task'=96,'x'=4,'core'=2] {'x','core'}, dimensions={0} | all-to-all | bytes 557056 | tf_op jit(solution)/shard_map/all_to_all | solution.py:410
  57.4 0.3 shard_map.96
  57.7 29.4 %all_to_all.16.recv_ref = bf16[96,8,128]{2,1,0:T(8,128)(2,1)S(1)} all-to-all(bf16[96,8,128]{2,1,0:T(8,128)(2,1)S(1)} %shard_map.96), channel_id=1, replica_groups=mesh['task'=96,'x'=4,'core'=2] {'task'}, dimensions={0} | all-to-all | bytes 393216 | tf_op jit(solution)/shard_map/all_to_all | solution.py:412
  87.1 0.9 shard_map.97
Async XLA Ops:
  0.0 8.2 %copy-start = (bf16[8,96,1024]{2,1,0:T(8,128)(2,1)S(1)}, bf16[8,96,1024]{2,1,0:T(8,128)(2,1)}, u32[]{:S(2)}) copy-start(bf16[8,96,1024]{2,1,0:T(8,128)(2,1)} %coeffs_ref.7) | copy-start | bytes 4718596
  0.0 1.0 %copy-start.1 = (bf16[64,1024]{1,0:T(8,128)(2,1)S(1)}, bf16[64,1024]{1,0:T(8,128)(2,1)}, u32[]{:S(2)}) copy-start(bf16[64,1024]{1,0:T(8,128)(2,1)} %d_ref.1) | copy-start | bytes 393220
  2.4 17.3 %all-to-all-start = ((bf16[4,64,8,128]{3,2,1,0:T(8,128)(2,1)}), bf16[4,64,8,128]{3,2,1,0:T(8,128)(2,1)S(1)}, u32[]{:S(2)}, u32[]{:S(2)}) async-start(bf16[4,64,8,128]{3,2,1,0:T(8,128)(2,1)} %shard_map.91), calls=%async_computation | async-start | bytes 1048576 | tf_op jit(solution)/shard_map/all_to_all | solution.py:400
  8.3 0.7 copy-start.2
  8.9 0.7 copy-start.3
  9.6 0.7 copy-start.4
  10.2 0.7 copy-start.5
  10.9 0.7 copy-start.6
  11.5 0.7 copy-start.7
  19.7 14.7 %collective-permute-start = (bf16[256,8,128]{2,1,0:T(8,128)(2,1)S(1)}, bf16[256,8,128]{2,1,0:T(8,128)(2,1)S(1)}, u32[]{:S(2)}, u32[]{:S(2)}) collective-permute-start(bf16[256,8,128]{2,1,0:T(8,128)(2,1)S(1)} %bitcast.4), channel_id=1, source_target_pairs={{0,1},{1,0},{2,3},{3,2},{4,5},{5,4},{6,7},{7,6},{8,9},{9,8},{10,11... | collective-permute-start | bytes 1572872 | tf_op jit(solution)/shard_map/ppermute | solution.py:407

commit v5 on v4

--- a/solution.py
+++ b/solution.py
@@ -28,8 +28,11 @@
     return jnp.where(mask, 1.0, 0.0).astype(BF)
 
 
-def pack_kernel(d_ref, out_ref, flat_ref):
+def pack_kernel(d_in, out_ref, flat_ref, d_ref, sem):
     blocks, cells = d_ref.shape
+    copy = pltpu.make_async_copy(d_in, d_ref, sem)
+    copy.start()
+    copy.wait()
     d = d_ref[...]
     for b in range(cells // 256):
         col = iota((1, 256), 1) + b * 256
@@ -50,11 +53,11 @@
     return pl.pallas_call(
         pack_kernel,
         out_shape=jax.ShapeDtypeStruct((peers, blocks, 8, 128), BF),
-        in_specs=[VM],
+        in_specs=[HB],
         out_specs=VM,
-        scratch_shapes=[pltpu.VMEM((blocks * 8, 128), F32)],
+        scratch_shapes=[pltpu.VMEM((blocks * 8, 128), F32), pltpu.VMEM(density.shape, BF), pltpu.SemaphoreType.DMA],
         compiler_params=pltpu.CompilerParams(vmem_limit_bytes=8 * MB),
-    )(density)
+    )(pltpu.with_memory_space_constraint(density, pltpu.HBM))
 
 
 def lane_move():
@@ -89,8 +92,8 @@
     return blocks
 
 
-def lefts_kernel(me_ref, owner_ref, slot_ref, left_ref, right_ref, aux_ref, dest_ref, coeffs_ref,
-                 l_out, table_ref, names_ref, count_ref, y0_ref, y1_ref, x0_ref, x1_ref, move_ref, lw_ref, l_ref, l_sem):
+def lefts_kernel(me_ref, owner_in, slot_in, left_in, right_in, aux_in, dest_in, coeffs_ref,
+                 l_out, table_ref, names_ref, owner_ref, slot_ref, left_ref, right_ref, aux_ref, dest_ref, i_sem, count_ref, y0_ref, y1_ref, x0_ref, x1_ref, move_ref, lw_ref, l_ref, l_sem):
     blocks, na, cells = coeffs_ref.shape
     tiles = na // 8
     tasks = slot_ref.shape[0]
@@ -98,9 +101,19 @@
     peers, cap = PEERS, 128 // PEERS
     sub, lane = iota((8, 128), 0), iota((8, 128), 1)
     me = me_ref[0]
+    indices = [
+        pltpu.make_async_copy(x_in, x_ref, i_sem.at[n])
+        for n, (x_in, x_ref) in enumerate(
+            ((owner_in, owner_ref), (slot_in, slot_ref), (left_in, left_ref), (right_in, right_ref), (aux_in, aux_ref), (dest_in, dest_ref))
+        )
+    ]
+    for copy in indices:
+        copy.start()
     for b in range(peers):
         count_ref[b] = 0
     move_ref[...] = lane_move()
+    for copy in indices:
+        copy.wait()
 
     def place_some(r, names):
         for u in range(share):
@@ -143,6 +156,7 @@
 def run_lefts(me, owner, slot, left, right, aux_of, dest, coeffs):
     blocks, na, cells = coeffs.shape
     tiles = na // 8
+    indices = [pltpu.with_memory_space_constraint(x, pltpu.HBM) for x in (owner, slot, left, right, aux_of, dest)]
     return pl.pallas_call(
         lefts_kernel,
         out_shape=(
@@ -150,9 +164,10 @@
             jax.ShapeDtypeStruct((1024,), jnp.int32),
             jax.ShapeDtypeStruct((8, 128), F32),
         ),
-        in_specs=[SM] * 7 + [VM],
+        in_specs=[SM] + [HB] * 6 + [VM],
         out_specs=(HB, SM, VM),
-        scratch_shapes=[
+        scratch_shapes=[pltpu.SMEM(x.shape, jnp.int32) for x in indices] + [
+            pltpu.SemaphoreType.DMA((6,)),
             pltpu.SMEM((PEERS,), jnp.int32),
             pltpu.VMEM((na * 8, 128), F32),
             pltpu.VMEM((na * 8, 128), F32),
@@ -164,7 +179,7 @@
             pltpu.SemaphoreType.DMA((tiles,)),
         ],
         compiler_params=pltpu.CompilerParams(vmem_limit_bytes=16 * MB),
-    )(me, owner, slot, left, right, aux_of, dest, coeffs)
+    )(me, *indices, coeffs)
 
 
 def multiply(coeffs_ref, coulomb_ref, r, y_ref):

time: 88.9 us -> 85.3 us (0.960)
  local copies, waits for them, and re-layouts: 5.96 us -> 1.01 us
  Pallas kernels: 24.5 us -> 25.9 us
    unnamed x16 -> x2, local copies, waits for them, and re-layouts: 4.95 us -> 0.01 us
    pallas_call x1, Pallas kernels: 1.35 us -> 2.37 us  [run_pack(): pl.pallas_call(pack_kernel, out_shape=jax.ShapeDtypeStruct((peers, blocks...]
  transfers between devices with their start and end apart: 2 -> 2, of which waited for: 0 -> 0; matrix products, arithmetic and copies ran while one was open for 1% -> 1% of each run, Pallas kernels for 12% -> 13%
where the time goes in v5:
time: 85.3 us; the launch traced here: 84.4 us
  blocking collectives  41.3 us (48%)
  Pallas kernels  25.9 us (30%)
  starting transfers between devices  16.1 us (19%)
  local copies, waits for them, and re-layouts  1.01 us (1%)
    all_to_all x1, blocking collectives, per_device(): back = lax.all_to_all(rows, 'task', 0, 0, tiled=True)  29.4 us
    all_to_all x1, blocking collectives, per_device(): recv = lax.all_to_all(send, BLK, 0, 0, tiled=True)  11.9 us
    ppermute x1, starting transfers between devices, per_device(): other = lax.ppermute(dens, 'core', [(0, 1), (1, 0)])  11.3 us
    pallas_call x1, Pallas kernels, run_tasks(): pl.pallas_call(tasks_kernel, out_shape=jax.ShapeDtypeStruct((peers, cap +...  11.1 us
    pallas_call x2, Pallas kernels, run_rights(): pl.pallas_call(functools.partial(rights_kernel, begin, end), out_shape=pl...  6.85 us
    all_to_all x1, starting transfers between devices, per_device(): dens = lax.all_to_all(run_pack(density, chips), 'x', 0, 0, tiled=True)  4.85 us
    pallas_call x1, Pallas kernels, run_lefts(): pl.pallas_call(lefts_kernel, out_shape=(pltpu.HBM((tiles * 256, blocks *...  4.43 us
    pallas_call x1, Pallas kernels, run_pack(): pl.pallas_call(pack_kernel, out_shape=jax.ShapeDtypeStruct((peers, blocks...  2.37 us
  transfers between devices with their start and end apart: 2, of which 0 were waited for; matrix products, arithmetic and copies ran while one was open for 1% of the time, Pallas kernels for 13%

profile of v5, /device:TPU:1, one launch (start us, length us, event | category | flops | bytes accessed | tf_op | source)
XLA Modules:
  0.0 84.4 jit_solution(1300538028246273670)
XLA Ops:
  0.0 0.0 copy-start
  0.0 2.4 %shard_map.91 = bf16[4,64,8,128]{3,2,1,0:T(8,128)(2,1)} custom-call(bf16[64,1024]{1,0:T(8,128)(2,1)} %d_in.1), custom_call_target="tpu_custom_call" | custom-call | tf_op jit(solution)/shard_map/pallas_call | solution.py:53
  2.4 4.9 %all-to-all-start = ((bf16[4,64,8,128]{3,2,1,0:T(8,128)(2,1)}), bf16[4,64,8,128]{3,2,1,0:T(8,128)(2,1)S(1)}, u32[]{:S(2)}, u32[]{:S(2)}) async-start(bf16[4,64,8,128]{3,2,1,0:T(8,128)(2,1)} %shard_map.91), calls=%async_computation | async-start | bytes 1048576 | tf_op jit(solution)/shard_map/all_to_all | solution.py:415
  7.2 1.0 %reshape.18.coulomb_ref = bf16[384,96]{1,0:T(8,128)(2,1)S(1)} reshape(bf16[4,9216]{1,0:T(4,128)(2,1)} %param.10) | data formatting | bytes 147456 | tf_op jit(solution)/shard_map/reshape | solution.py:417
  8.3 0.0 copy-done
  8.3 4.4 %shard_map.92 = (bf16[3072,256]{1,0:T(8,128)(2,1)}, s32[1024]{0:T(1024)S(1)}, f32[8,128]{1,0:T(8,128)S(1)}) custom-call(s32[1]{0:T(128)} %bitcast.1.me_ref, s32[64]{0:T(128)} %bitcast.7, s32[64]{0:T(128)} %slot_in.1, s32[64]{0:T(128)} %left_in.1, s32[64]{0:T(128)} %right_in.1, s32[64]{0:T(128)} %aux_in.1, s32[64]{0:T(128)} %dest_in.1, ...), custom_call_target="tpu_custom_call" | custom-call | tf_op jit(solution)/shard_map/pallas_call | solution.py:160
  12.7 3.4 %shard_map.93.w1_in = bf16[12,384,256]{2,1,0:T(8,128)(2,1)} custom-call(bf16[8,96,1024]{2,1,0:T(8,128)(2,1)S(1)} %copy-done, bf16[384,96]{1,0:T(8,128)(2,1)S(1)} %reshape.18.coulomb_ref, f32[8,128]{1,0:T(8,128)S(1)} %get-tuple-element.17.after_ref.names_ref), custom_call_target="tpu_custom_call" | custom-call | tf_op jit(solution)/shard_map/pallas_call | solution.py:234
  16.1 0.0 all-to-all-done
  16.2 11.3 %collective-permute-start = (bf16[256,8,128]{2,1,0:T(8,128)(2,1)S(1)}, bf16[256,8,128]{2,1,0:T(8,128)(2,1)S(1)}, u32[]{:S(2)}, u32[]{:S(2)}) collective-permute-start(bf16[256,8,128]{2,1,0:T(8,128)(2,1)S(1)} %bitcast.4), channel_id=1, source_target_pairs={{0,1},{1,0},{2,3},{3,2},{4,5},{5,4},{6,7},{7,6},{8,9},{9,8},{10,11... | collective-permute-start | bytes 1572872 | tf_op jit(solution)/shard_map/ppermute | solution.py:422
  27.4 3.4 %shard_map.94.w2_in = bf16[12,384,256]{2,1,0:T(8,128)(2,1)} custom-call(bf16[8,96,1024]{2,1,0:T(8,128)(2,1)S(1)} %copy-done, bf16[384,96]{1,0:T(8,128)(2,1)S(1)} %reshape.18.coulomb_ref, bf16[256,8,128]{2,1,0:T(8,128)(2,1)S(1)} %bitcast.5), custom_call_target="tpu_custom_call" | custom-call | tf_op jit(solution)/shard_map/pallas_call | solution.py:234
  30.8 0.0 collective-permute-done.e_ref
  30.9 11.1 %shard_map.95 = bf16[8,17,8,128]{3,2,1,0:T(8,128)(2,1)S(1)} custom-call(s32[1024]{0:T(1024)S(1)} %get-tuple-element.16.table_ref, f32[8,128]{1,0:T(8,128)S(1)} %get-tuple-element.17.after_ref.names_ref, bf16[8,96,1024]{2,1,0:T(8,128)(2,1)S(1)} %copy-done, bf16[384,96]{1,0:T(8,128)(2,1)S(1)} %reshape.18.coulomb_ref, bf16[12,384,256]{2,1,0:T(8,128)(2,1)} %shard_map.93.w1_in, ...), custom_call_target="tpu_custom_call" | custom-call | tf_op jit(solution)/shard_map/pallas_call | solution.py:329
  42.0 11.9 %all_to_all.15.recv_ref = bf16[8,17,8,128]{3,2,1,0:T(8,128)(2,1)S(1)} all-to-all(bf16[8,17,8,128]{3,2,1,0:T(8,128)(2,1)S(1)} %shard_map.95), channel_id=1, replica_groups=mesh['task'=96,'x'=4,'core'=2] {'x','core'}, dimensions={0} | all-to-all | bytes 557056 | tf_op jit(solution)/shard_map/all_to_all | solution.py:425
  53.9 0.3 shard_map.96
  54.2 29.4 %all_to_all.16.recv_ref = bf16[96,8,128]{2,1,0:T(8,128)(2,1)S(1)} all-to-all(bf16[96,8,128]{2,1,0:T(8,128)(2,1)S(1)} %shard_map.96), channel_id=1, replica_groups=mesh['task'=96,'x'=4,'core'=2] {'task'}, dimensions={0} | all-to-all | bytes 393216 | tf_op jit(solution)/shard_map/all_to_all | solution.py:427
  83.6 0.9 %shard_map.97 = f32[8,128]{1,0:T(8,128)} custom-call(bf16[96,8,128]{2,1,0:T(8,128)(2,1)S(1)} %all_to_all.16.recv_ref), custom_call_target="tpu_custom_call" | custom-call | tf_op jit(solution)/shard_map/pallas_call | solution.py:402
Async XLA Ops:
  0.0 8.3 %copy-start = (bf16[8,96,1024]{2,1,0:T(8,128)(2,1)S(1)}, bf16[8,96,1024]{2,1,0:T(8,128)(2,1)}, u32[]{:S(2)}) copy-start(bf16[8,96,1024]{2,1,0:T(8,128)(2,1)} %coeffs_ref.7) | copy-start | bytes 4718596
  2.4 13.8 %all-to-all-start = ((bf16[4,64,8,128]{3,2,1,0:T(8,128)(2,1)}), bf16[4,64,8,128]{3,2,1,0:T(8,128)(2,1)S(1)}, u32[]{:S(2)}, u32[]{:S(2)}) async-start(bf16[4,64,8,128]{3,2,1,0:T(8,128)(2,1)} %shard_map.91), calls=%async_computation | async-start | bytes 1048576 | tf_op jit(solution)/shard_map/all_to_all | solution.py:415
  16.2 14.7 %collective-permute-start = (bf16[256,8,128]{2,1,0:T(8,128)(2,1)S(1)}, bf16[256,8,128]{2,1,0:T(8,128)(2,1)S(1)}, u32[]{:S(2)}, u32[]{:S(2)}) collective-permute-start(bf16[256,8,128]{2,1,0:T(8,128)(2,1)S(1)} %bitcast.4), channel_id=1, source_target_pairs={{0,1},{1,0},{2,3},{3,2},{4,5},{5,4},{6,7},{7,6},{8,9},{9,8},{10,11... | collective-permute-start | bytes 1572872 | tf_op jit(solution)/shard_map/ppermute | solution.py:422

commit v6 on v5

--- a/solution.py
+++ b/solution.py
@@ -1,4 +1,5 @@
 import functools
+import math
 
 import jax
 import jax.numpy as jnp
@@ -17,7 +18,7 @@
 CORES = 2
 HELD = 64
 AUX = 4
-CUT1, CUT2 = 3, 6
+CUT1, CUT2 = 3, 7
 
 
 def iota(shape, dim):
@@ -28,19 +29,21 @@
     return jnp.where(mask, 1.0, 0.0).astype(BF)
 
 
-def pack_kernel(d_in, out_ref, flat_ref, d_ref, sem):
+def pack_kernel(d_in, out_ref, flat_ref, d_ref, move_ref, sem):
     blocks, cells = d_ref.shape
     copy = pltpu.make_async_copy(d_in, d_ref, sem)
     copy.start()
+    for a in range(cells // 256):
+        for b in range(cells // 256):
+            col = iota((1, 256), 1) + b * 256
+            source = ((col & 31) << 5) + (col >> 5) - a * 256
+            move_ref[a * 4 + b] = ones_where(iota((256, 256), 0) == source)
     copy.wait()
     d = d_ref[...]
     for b in range(cells // 256):
-        col = iota((1, 256), 1) + b * 256
-        source = ((col & 31) << 5) + (col >> 5)
         y = jnp.zeros((blocks, 256), F32)
         for a in range(cells // 256):
-            move = ones_where(iota((256, 256), 0) == source - a * 256)
-            y += jnp.dot(d[:, a * 256:(a + 1) * 256], move, preferred_element_type=F32)
+            y += jnp.dot(d[:, a * 256:(a + 1) * 256], move_ref[a * 4 + b], preferred_element_type=F32)
         for e in range(2):
             flat_ref[pl.ds(2 * b + e, blocks, stride=8), :] = y[:, e * 128:(e + 1) * 128]
     x = flat_ref[...].reshape(blocks, 8, 128).astype(BF)
@@ -55,7 +58,8 @@
         out_shape=jax.ShapeDtypeStruct((peers, blocks, 8, 128), BF),
         in_specs=[HB],
         out_specs=VM,
-        scratch_shapes=[pltpu.VMEM((blocks * 8, 128), F32), pltpu.VMEM(density.shape, BF), pltpu.SemaphoreType.DMA],
+        scratch_shapes=[pltpu.VMEM((blocks * 8, 128), F32), pltpu.VMEM(density.shape, BF),
+                        pltpu.VMEM((16, 256, 256), BF), pltpu.SemaphoreType.DMA],
         compiler_params=pltpu.CompilerParams(vmem_limit_bytes=8 * MB),
     )(pltpu.with_memory_space_constraint(density, pltpu.HBM))
 
@@ -92,7 +96,7 @@
     return blocks
 
 
-def lefts_kernel(me_ref, owner_in, slot_in, left_in, right_in, aux_in, dest_in, coeffs_ref,
+def lefts_kernel(deep, wide, me_ref, owner_in, slot_in, left_in, right_in, aux_in, dest_in, coeffs_ref,
                  l_out, table_ref, names_ref, owner_ref, slot_ref, left_ref, right_ref, aux_ref, dest_ref, i_sem, count_ref, y0_ref, y1_ref, x0_ref, x1_ref, move_ref, lw_ref, l_ref, l_sem):
     blocks, na, cells = coeffs_ref.shape
     tiles = na // 8
@@ -127,7 +131,8 @@
             table_ref[tasks + t] = right_ref[t] * AUX + aux_ref[t]
             table_ref[2 * tasks + t] = left_ref[t]
             table_ref[3 * tasks + t] = peer * (cap + 1) + place
-            name = (dest // peers + 1).astype(F32)
+            task = lax.div(dest, peers)
+            name = (lax.rem(task, wide) * deep + lax.div(task, wide) + 1).astype(F32)
             names = jnp.where((sub == peer) & (lane == me * cap + place), name, names)
         return names
 
@@ -153,12 +158,12 @@
         copy.wait()
 
 
-def run_lefts(me, owner, slot, left, right, aux_of, dest, coeffs):
+def run_lefts(deep, wide, me, owner, slot, left, right, aux_of, dest, coeffs):
     blocks, na, cells = coeffs.shape
     tiles = na // 8
     indices = [pltpu.with_memory_space_constraint(x, pltpu.HBM) for x in (owner, slot, left, right, aux_of, dest)]
     return pl.pallas_call(
-        lefts_kernel,
+        functools.partial(lefts_kernel, deep, wide),
         out_shape=(
             pltpu.HBM((tiles * 256, blocks * 32), BF),
             jax.ShapeDtypeStruct((1024,), jnp.int32),
@@ -244,6 +249,32 @@
     )(coeffs, vall, after)
 
 
+def near_kernel(begin, end, coeffs_ref, coulomb_ref, after_ref, w_ref, y0_ref, y1_ref, x0_ref, x1_ref, move_ref):
+    na = coeffs_ref.shape[1]
+    aux = coulomb_ref.shape[0] // na
+    move_ref[...] = lane_move()
+    ys, xs = (y0_ref, y1_ref), (x0_ref, x1_ref)
+    multiply(coeffs_ref, coulomb_ref, begin, ys[0])
+    for r in range(begin, end):
+        e = (r - begin) % 2
+        if r + 1 < end:
+            multiply(coeffs_ref, coulomb_ref, r + 1, ys[1 - e])
+        turn(ys[e], xs[e], move_ref, w_ref, (r - begin) * aux, na // 8)
+
+
+def run_near(coeffs, vall, after, begin, end):
+    na = coeffs.shape[1]
+    aux = vall.shape[0] // na
+    return pl.pallas_call(
+        functools.partial(near_kernel, begin, end),
+        out_shape=jax.ShapeDtypeStruct(((end - begin) * aux, na // 8 * 32, 256), BF),
+        in_specs=[VM, VM, pl.BlockSpec(memory_space=pl.ANY)],
+        out_specs=VM,
+        scratch_shapes=rights_scratch(vall.shape[0]),
+        compiler_params=pltpu.CompilerParams(vmem_limit_bytes=20 * MB),
+    )(coeffs, vall, after)
+
+
 def tasks_kernel(table_ref, names_ref, coeffs_ref, coulomb_ref, w1_in, w2_in, l_in, d_ref, e_ref,
                  out_ref, y0_ref, y1_ref, x0_ref, x1_ref, move_ref, dl_ref, a_ref, send_ref, w_ref, l_ref, sem):
     tiles = l_ref.shape[0] // 256
@@ -261,7 +292,7 @@
         pltpu.make_async_copy(w1_in, w_ref.at[here], sem.at[1]),
         pltpu.make_async_copy(w2_in, w_ref.at[there], sem.at[2]),
     ]
-    for i in (1, 2, 0):
+    for i in (1, 0, 2):
         copies[i].start()
     move_ref[...] = lane_move()
     ys, xs = (y0_ref, y1_ref), (x0_ref, x1_ref)
@@ -324,12 +355,12 @@
 
 
 def run_tasks(table, names, coeffs, vall, w1, w2, l, dens, other, tasks, peers, cap):
-    w1, w2, l = (pltpu.with_memory_space_constraint(x, pltpu.HBM) for x in (w1, w2, l))
+    w1, l = (pltpu.with_memory_space_constraint(x, pltpu.HBM) for x in (w1, l))
     blocks, na, _ = coeffs.shape
     return pl.pallas_call(
         tasks_kernel,
         out_shape=jax.ShapeDtypeStruct((peers, cap + 1, 8, 128), BF),
-        in_specs=[SM, VM, VM, VM, HB, HB, HB, VM, VM],
+        in_specs=[SM, VM, VM, VM, HB, pl.BlockSpec(memory_space=pl.ANY), HB, VM, VM],
         out_specs=VM,
         scratch_shapes=rights_scratch(vall.shape[0]) + [
             pltpu.VMEM((tasks * 32, 256), BF),
@@ -410,21 +441,21 @@
 
 def per_device(coeffs, coulomb, density, task_owner, task_slot, task_left, task_right, task_aux, task_dest):
     na = coeffs.shape[1]
-    blk, task = lax.axis_size("x") * lax.axis_size("core"), lax.axis_size("task")
+    blk, task = lax.axis_size("x") * lax.axis_size("core"), lax.axis_size("z") * lax.axis_size("y")
     chips = blk // CORES
     dens = lax.all_to_all(run_pack(density, chips), "x", 0, 0, tiled=True)
     me = lax.axis_index(BLK).astype(jnp.int32).reshape(1)
     vall = coulomb.reshape(coulomb.shape[0] * na, na)
-    l, table, names = run_lefts(me, task_owner.reshape(-1), task_slot, task_left, task_right, task_aux, task_dest, coeffs)
+    l, table, names = run_lefts(lax.axis_size("z"), lax.axis_size("y"), me, task_owner.reshape(-1), task_slot, task_left, task_right, task_aux, task_dest, coeffs)
     w1 = run_rights(coeffs, vall, names, 0, CUT1)
     dens = dens.reshape(chips * HELD, 8, 128)
     dens, l, table, names, w1 = lax.optimization_barrier((dens, l, table, names, w1))
     other = lax.ppermute(dens, "core", [(0, 1), (1, 0)])
-    w2 = run_rights(coeffs, vall, dens, CUT1, CUT2)
+    w2 = run_near(coeffs, vall, dens, CUT1, CUT2)
     send = run_tasks(table, names, coeffs, vall, w1, w2, l, dens, other, task_slot.shape[0], blk, 128 // blk)
     recv = lax.all_to_all(send, BLK, 0, 0, tiled=True)
     rows = run_spread(recv, task, BF)
-    back = lax.all_to_all(rows, "task", 0, 0, tiled=True)
+    back = lax.all_to_all(rows, ("y", "z"), 0, 0, tiled=True)
     return run_final(back).reshape(1, density.shape[1])
 
 
@@ -432,8 +463,9 @@
 
 
 def solution(mesh):
-    sizes = (mesh.shape["task"], mesh.shape["blk"] // CORES, CORES)
-    fine = jax.sharding.Mesh(mesh.devices.reshape(sizes), ("task", "x", "core"))
-    every = P(("task", "x", "core"))
+    wide = math.gcd(mesh.shape["task"], 8)
+    sizes = (mesh.shape["task"] // wide, wide, mesh.shape["blk"] // CORES, CORES)
+    fine = jax.sharding.Mesh(mesh.devices.reshape(sizes), ("z", "y", "x", "core"))
+    every = P(("z", "y", "x", "core"))
     placed = (every, every, P(BLK), every, every, every, every, every, every)
     return jax.shard_map(per_device, mesh=fine, in_specs=placed, out_specs=every, check_vma=False)

time: 85.3 us -> 83.8 us (0.982)
  the two profiles are of different devices: /device:TPU:1 before, /device:TPU:8 now
where the time goes in v6:
time: 83.8 us; the launch traced here: 83.5 us
  blocking collectives  50.6 us (60%)
  Pallas kernels  24.8 us (30%)
  starting transfers between devices  6.39 us (8%)
  local copies, waits for them, and re-layouts  1.01 us (1%)
    all_to_all x1, blocking collectives, per_device(): back = lax.all_to_all(rows, ('y', 'z'), 0, 0, tiled=True)  38.7 us
    all_to_all x1, blocking collectives, per_device(): recv = lax.all_to_all(send, BLK, 0, 0, tiled=True)  11.9 us
    pallas_call x1, Pallas kernels, run_tasks(): pl.pallas_call(tasks_kernel, out_shape=jax.ShapeDtypeStruct((peers, cap +...  10.2 us
    pallas_call x1, Pallas kernels, run_lefts(): pl.pallas_call(functools.partial(lefts_kernel, deep, wide), out_shape=(pl...  4.44 us
    all_to_all x1, starting transfers between devices, per_device(): dens = lax.all_to_all(run_pack(density, chips), 'x', 0, 0, tiled=True)  4.3 us
    pallas_call x1, Pallas kernels, run_rights(): pl.pallas_call(functools.partial(rights_kernel, begin, end), out_shape=pl...  3.43 us
    pallas_call x1, Pallas kernels, run_near(): pl.pallas_call(functools.partial(near_kernel, begin, end), out_shape=jax....  3.29 us
    pallas_call x1, Pallas kernels, run_pack(): pl.pallas_call(pack_kernel, out_shape=jax.ShapeDtypeStruct((peers, blocks...  2.34 us
  transfers between devices with their start and end apart: 2, of which 1 were waited for; matrix products, arithmetic and copies ran while one was open for 1% of the time, Pallas kernels for 13%

profile of v6, /device:TPU:8, one launch (start us, length us, event | category | flops | bytes accessed | tf_op | source)
XLA Modules:
  0.0 83.5 jit_solution(4790573470074874050)
XLA Ops:
  0.0 0.0 copy-start
  0.0 2.3 %shard_map.91 = bf16[4,64,8,128]{3,2,1,0:T(8,128)(2,1)} custom-call(bf16[64,1024]{1,0:T(8,128)(2,1)} %d_in.1), custom_call_target="tpu_custom_call" | custom-call | tf_op jit(solution)/shard_map/pallas_call | solution.py:56
  2.3 4.3 %all-to-all-start = ((bf16[4,64,8,128]{3,2,1,0:T(8,128)(2,1)}), bf16[4,64,8,128]{3,2,1,0:T(8,128)(2,1)S(1)}, u32[]{:S(2)}, u32[]{:S(2)}) async-start(bf16[4,64,8,128]{3,2,1,0:T(8,128)(2,1)} %shard_map.91), calls=%async_computation | async-start | bytes 1048576 | tf_op jit(solution)/shard_map/all_to_all | solution.py:446
  6.7 1.0 %reshape.18.coulomb_ref = bf16[384,96]{1,0:T(8,128)(2,1)S(1)} reshape(bf16[4,9216]{1,0:T(4,128)(2,1)} %param.10) | data formatting | bytes 147456 | tf_op jit(solution)/shard_map/reshape | solution.py:448
  7.7 0.0 copy-done
  7.7 4.4 %shard_map.92 = (bf16[3072,256]{1,0:T(8,128)(2,1)}, s32[1024]{0:T(1024)S(1)}, f32[8,128]{1,0:T(8,128)S(1)}) custom-call(s32[1]{0:T(128)} %bitcast.1.me_ref, s32[64]{0:T(128)} %bitcast.7, s32[64]{0:T(128)} %slot_in.1, s32[64]{0:T(128)} %left_in.1, s32[64]{0:T(128)} %right_in.1, s32[64]{0:T(128)} %aux_in.1, s32[64]{0:T(128)} %dest_in.1, ...), custom_call_target="tpu_custom_call" | custom-call | tf_op jit(solution)/shard_map/pallas_call | solution.py:165
  12.1 3.4 %shard_map.93.w1_in = bf16[12,384,256]{2,1,0:T(8,128)(2,1)} custom-call(bf16[8,96,1024]{2,1,0:T(8,128)(2,1)S(1)} %copy-done, bf16[384,96]{1,0:T(8,128)(2,1)S(1)} %reshape.18.coulomb_ref, f32[8,128]{1,0:T(8,128)S(1)} %get-tuple-element.17.after_ref.names_ref), custom_call_target="tpu_custom_call" | custom-call | tf_op jit(solution)/shard_map/pallas_call | solution.py:239
  15.6 0.6 all-to-all-done
  16.1 2.1 %collective-permute-start = (bf16[256,8,128]{2,1,0:T(8,128)(2,1)S(1)}, bf16[256,8,128]{2,1,0:T(8,128)(2,1)S(1)}, u32[]{:S(2)}, u32[]{:S(2)}) collective-permute-start(bf16[256,8,128]{2,1,0:T(8,128)(2,1)S(1)} %bitcast.4), channel_id=1, source_target_pairs={{0,1},{1,0},{2,3},{3,2},{4,5},{5,4},{6,7},{7,6},{8,9},{9,8},{10,11... | collective-permute-start | bytes 1572872 | tf_op jit(solution)/shard_map/ppermute | solution.py:453
  18.2 3.3 %shard_map.94.w2_in = bf16[16,384,256]{2,1,0:T(8,128)(2,1)S(1)} custom-call(bf16[8,96,1024]{2,1,0:T(8,128)(2,1)S(1)} %copy-done, bf16[384,96]{1,0:T(8,128)(2,1)S(1)} %reshape.18.coulomb_ref, bf16[256,8,128]{2,1,0:T(8,128)(2,1)S(1)} %bitcast.5), custom_call_target="tpu_custom_call" | custom-call | tf_op jit(solution)/shard_map/pallas_call | solution.py:268
  21.5 0.0 collective-permute-done.e_ref
  21.5 10.2 %shard_map.95 = bf16[8,17,8,128]{3,2,1,0:T(8,128)(2,1)S(1)} custom-call(s32[1024]{0:T(1024)S(1)} %get-tuple-element.16.table_ref, f32[8,128]{1,0:T(8,128)S(1)} %get-tuple-element.17.after_ref.names_ref, bf16[8,96,1024]{2,1,0:T(8,128)(2,1)S(1)} %copy-done, bf16[384,96]{1,0:T(8,128)(2,1)S(1)} %reshape.18.coulomb_ref, bf16[12,384,256]{2,1,0:T(8,128)(2,1)} %shard_map.93.w1_in, ...), custom_call_target="tpu_custom_call" | custom-call | tf_op jit(solution)/shard_map/pallas_call | solution.py:360
  31.7 11.9 %all_to_all.15.recv_ref = bf16[8,17,8,128]{3,2,1,0:T(8,128)(2,1)S(1)} all-to-all(bf16[8,17,8,128]{3,2,1,0:T(8,128)(2,1)S(1)} %shard_map.95), channel_id=1, replica_groups=mesh['z'=12,'y'=8,'x'=4,'core'=2] {'x','core'}, dimensions={0} | all-to-all | bytes 557056 | tf_op jit(solution)/shard_map/all_to_all | solution.py:456
  43.6 0.3 shard_map.96
  43.9 38.7 %all_to_all.16.recv_ref = bf16[96,8,128]{2,1,0:T(8,128)(2,1)S(1)} all-to-all(bf16[96,8,128]{2,1,0:T(8,128)(2,1)S(1)} %shard_map.96), channel_id=1, replica_groups=mesh['z'=12,'y'=8,'x'=4,'core'=2] {'y','z'}, dimensions={0} | all-to-all | bytes 393216 | tf_op jit(solution)/shard_map/all_to_all | solution.py:458
  82.6 0.9 %shard_map.97 = f32[8,128]{1,0:T(8,128)} custom-call(bf16[96,8,128]{2,1,0:T(8,128)(2,1)S(1)} %all_to_all.16.recv_ref), custom_call_target="tpu_custom_call" | custom-call | tf_op jit(solution)/shard_map/pallas_call | solution.py:433
Async XLA Ops:
  0.0 7.7 %copy-start = (bf16[8,96,1024]{2,1,0:T(8,128)(2,1)S(1)}, bf16[8,96,1024]{2,1,0:T(8,128)(2,1)}, u32[]{:S(2)}) copy-start(bf16[8,96,1024]{2,1,0:T(8,128)(2,1)} %coeffs_ref.7) | copy-start | bytes 4718596
  2.3 13.8 %all-to-all-start = ((bf16[4,64,8,128]{3,2,1,0:T(8,128)(2,1)}), bf16[4,64,8,128]{3,2,1,0:T(8,128)(2,1)S(1)}, u32[]{:S(2)}, u32[]{:S(2)}) async-start(bf16[4,64,8,128]{3,2,1,0:T(8,128)(2,1)} %shard_map.91), calls=%async_computation | async-start | bytes 1048576 | tf_op jit(solution)/shard_map/all_to_all | solution.py:446
  16.1 5.4 %collective-permute-start = (bf16[256,8,128]{2,1,0:T(8,128)(2,1)S(1)}, bf16[256,8,128]{2,1,0:T(8,128)(2,1)S(1)}, u32[]{:S(2)}, u32[]{:S(2)}) collective-permute-start(bf16[256,8,128]{2,1,0:T(8,128)(2,1)S(1)} %bitcast.4), channel_id=1, source_target_pairs={{0,1},{1,0},{2,3},{3,2},{4,5},{5,4},{6,7},{7,6},{8,9},{9,8},{10,11... | collective-permute-start | bytes 1572872 | tf_op jit(solution)/shard_map/ppermute | solution.py:453

commit v7 on v6

--- a/solution.py
+++ b/solution.py
@@ -417,6 +417,24 @@
     return out
 
 
+def halfway_kernel(recv_ref, out_ref):
+    deep = out_ref.shape[0]
+    total = recv_ref[0:deep].astype(F32)
+    for y in range(1, recv_ref.shape[0] // deep):
+        total = total + recv_ref[y * deep:(y + 1) * deep].astype(F32)
+    out_ref[...] = total
+
+
+def run_halfway(recv, wide):
+    return pl.pallas_call(
+        halfway_kernel,
+        out_shape=jax.ShapeDtypeStruct((recv.shape[0] // wide, 8, 128), F32),
+        in_specs=[VM],
+        out_specs=VM,
+        compiler_params=pltpu.CompilerParams(vmem_limit_bytes=4 * MB),
+    )(recv)
+
+
 def final_kernel(recv_ref, out_ref):
     total = jnp.sum(recv_ref[...].astype(F32), axis=0) * -0.25
     vi = iota((64, 128), 0) >> 3
@@ -455,7 +473,8 @@
     send = run_tasks(table, names, coeffs, vall, w1, w2, l, dens, other, task_slot.shape[0], blk, 128 // blk)
     recv = lax.all_to_all(send, BLK, 0, 0, tiled=True)
     rows = run_spread(recv, task, BF)
-    back = lax.all_to_all(rows, ("y", "z"), 0, 0, tiled=True)
+    back = run_halfway(lax.all_to_all(rows, "y", 0, 0, tiled=True), lax.axis_size("y"))
+    back = lax.all_to_all(back, "z", 0, 0, tiled=True)
     return run_final(back).reshape(1, density.shape[1])
 
 

time: 83.8 us -> 87.5 us (1.044)
  the two profiles are of different devices: /device:TPU:8 before, /device:TPU:1 now
where the time goes in v7:
time: 87.5 us; the launch traced here: 86.1 us
  blocking collectives  44.1 us (50%)
  Pallas kernels  24.7 us (28%)
  starting transfers between devices  16.1 us (18%)
  local copies, waits for them, and re-layouts  1.01 us (1%)
    all_to_all x1, blocking collectives, per_device(): back = lax.all_to_all(back, 'z', 0, 0, tiled=True)  20.1 us
    all_to_all x1, blocking collectives, per_device(): lax.all_to_all(rows, 'y', 0, 0, tiled=True)  12.1 us
    all_to_all x1, blocking collectives, per_device(): recv = lax.all_to_all(send, BLK, 0, 0, tiled=True)  11.9 us
    ppermute x1, starting transfers between devices, per_device(): other = lax.ppermute(dens, 'core', [(0, 1), (1, 0)])  11.2 us
    pallas_call x1, Pallas kernels, run_tasks(): pl.pallas_call(tasks_kernel, out_shape=jax.ShapeDtypeStruct((peers, cap +...  10.2 us
    all_to_all x1, starting transfers between devices, per_device(): dens = lax.all_to_all(run_pack(density, chips), 'x', 0, 0, tiled=True)  4.85 us
    pallas_call x1, Pallas kernels, run_lefts(): pl.pallas_call(functools.partial(lefts_kernel, deep, wide), out_shape=(pl...  4.44 us
    pallas_call x1, Pallas kernels, run_rights(): pl.pallas_call(functools.partial(rights_kernel, begin, end), out_shape=pl...  3.43 us
  transfers between devices with their start and end apart: 2, of which 0 were waited for; matrix products, arithmetic and copies ran while one was open for 1% of the time, Pallas kernels for 13%

profile of v7, /device:TPU:1, one launch (start us, length us, event | category | flops | bytes accessed | tf_op | source)
XLA Modules:
  0.0 86.1 jit_solution(12430380856996636931)
XLA Ops:
  0.0 0.0 copy-start
  0.0 2.3 %shard_map.91 = bf16[4,64,8,128]{3,2,1,0:T(8,128)(2,1)} custom-call(bf16[64,1024]{1,0:T(8,128)(2,1)} %d_in.1), custom_call_target="tpu_custom_call" | custom-call | tf_op jit(solution)/shard_map/pallas_call | solution.py:56
  2.3 4.9 %all-to-all-start = ((bf16[4,64,8,128]{3,2,1,0:T(8,128)(2,1)}), bf16[4,64,8,128]{3,2,1,0:T(8,128)(2,1)S(1)}, u32[]{:S(2)}, u32[]{:S(2)}) async-start(bf16[4,64,8,128]{3,2,1,0:T(8,128)(2,1)} %shard_map.91), calls=%async_computation | async-start | bytes 1048576 | tf_op jit(solution)/shard_map/all_to_all | solution.py:464
  7.2 1.0 %reshape.18.coulomb_ref = bf16[384,96]{1,0:T(8,128)(2,1)S(1)} reshape(bf16[4,9216]{1,0:T(4,128)(2,1)} %param.10) | data formatting | bytes 147456 | tf_op jit(solution)/shard_map/reshape | solution.py:466
  8.2 0.0 copy-done
  8.2 4.4 %shard_map.92 = (bf16[3072,256]{1,0:T(8,128)(2,1)}, s32[1024]{0:T(1024)S(1)}, f32[8,128]{1,0:T(8,128)S(1)}) custom-call(s32[1]{0:T(128)} %bitcast.1.me_ref, s32[64]{0:T(128)} %bitcast.7, s32[64]{0:T(128)} %slot_in.1, s32[64]{0:T(128)} %left_in.1, s32[64]{0:T(128)} %right_in.1, s32[64]{0:T(128)} %aux_in.1, s32[64]{0:T(128)} %dest_in.1, ...), custom_call_target="tpu_custom_call" | custom-call | tf_op jit(solution)/shard_map/pallas_call | solution.py:165
  12.7 3.4 %shard_map.93.w1_in = bf16[12,384,256]{2,1,0:T(8,128)(2,1)} custom-call(bf16[8,96,1024]{2,1,0:T(8,128)(2,1)S(1)} %copy-done, bf16[384,96]{1,0:T(8,128)(2,1)S(1)} %reshape.18.coulomb_ref, f32[8,128]{1,0:T(8,128)S(1)} %get-tuple-element.17.after_ref.names_ref), custom_call_target="tpu_custom_call" | custom-call | tf_op jit(solution)/shard_map/pallas_call | solution.py:239
  16.1 0.0 all-to-all-done
  16.1 11.2 %collective-permute-start = (bf16[256,8,128]{2,1,0:T(8,128)(2,1)S(1)}, bf16[256,8,128]{2,1,0:T(8,128)(2,1)S(1)}, u32[]{:S(2)}, u32[]{:S(2)}) collective-permute-start(bf16[256,8,128]{2,1,0:T(8,128)(2,1)S(1)} %bitcast.4), channel_id=1, source_target_pairs={{0,1},{1,0},{2,3},{3,2},{4,5},{5,4},{6,7},{7,6},{8,9},{9,8},{10,11... | collective-permute-start | bytes 1572872 | tf_op jit(solution)/shard_map/ppermute | solution.py:471
  27.4 3.3 %shard_map.94.w2_in = bf16[16,384,256]{2,1,0:T(8,128)(2,1)S(1)} custom-call(bf16[8,96,1024]{2,1,0:T(8,128)(2,1)S(1)} %copy-done, bf16[384,96]{1,0:T(8,128)(2,1)S(1)} %reshape.18.coulomb_ref, bf16[256,8,128]{2,1,0:T(8,128)(2,1)S(1)} %bitcast.5), custom_call_target="tpu_custom_call" | custom-call | tf_op jit(solution)/shard_map/pallas_call | solution.py:268
  30.7 0.0 collective-permute-done.e_ref
  30.7 10.2 %shard_map.95 = bf16[8,17,8,128]{3,2,1,0:T(8,128)(2,1)S(1)} custom-call(s32[1024]{0:T(1024)S(1)} %get-tuple-element.16.table_ref, f32[8,128]{1,0:T(8,128)S(1)} %get-tuple-element.17.after_ref.names_ref, bf16[8,96,1024]{2,1,0:T(8,128)(2,1)S(1)} %copy-done, bf16[384,96]{1,0:T(8,128)(2,1)S(1)} %reshape.18.coulomb_ref, bf16[12,384,256]{2,1,0:T(8,128)(2,1)} %shard_map.93.w1_in, ...), custom_call_target="tpu_custom_call" | custom-call | tf_op jit(solution)/shard_map/pallas_call | solution.py:360
  40.9 11.9 %all_to_all.20.recv_ref = bf16[8,17,8,128]{3,2,1,0:T(8,128)(2,1)S(1)} all-to-all(bf16[8,17,8,128]{3,2,1,0:T(8,128)(2,1)S(1)} %shard_map.95), channel_id=1, replica_groups=mesh['z'=12,'y'=8,'x'=4,'core'=2] {'x','core'}, dimensions={0} | all-to-all | bytes 557056 | tf_op jit(solution)/shard_map/all_to_all | solution.py:474
  52.8 0.3 shard_map.96
  53.1 12.1 %all_to_all.21.recv_ref = bf16[96,8,128]{2,1,0:T(8,128)(2,1)S(1)} all-to-all(bf16[96,8,128]{2,1,0:T(8,128)(2,1)S(1)} %shard_map.96), channel_id=1, replica_groups=mesh['z'=12,'y'=8,'x'=4,'core'=2] {'y'}, dimensions={0} | all-to-all | bytes 393216 | tf_op jit(solution)/shard_map/all_to_all | solution.py:476
  65.2 20.1 %all_to_all.22.recv_ref = f32[12,8,128]{2,1,0:T(8,128)S(1)} all-to-all(f32[12,8,128]{2,1,0:T(8,128)S(1)} %shard_map.97), channel_id=1, replica_groups=mesh['z'=12,'y'=8,'x'=4,'core'=2] {'z'}, dimensions={0} | all-to-all | bytes 98304 | tf_op jit(solution)/shard_map/all_to_all | solution.py:477
  85.3 0.8 shard_map.98
  (1 shorter events, 0.0 us)
Async XLA Ops:
  0.0 8.2 %copy-start = (bf16[8,96,1024]{2,1,0:T(8,128)(2,1)S(1)}, bf16[8,96,1024]{2,1,0:T(8,128)(2,1)}, u32[]{:S(2)}) copy-start(bf16[8,96,1024]{2,1,0:T(8,128)(2,1)} %coeffs_ref.7) | copy-start | bytes 4718596
  2.3 13.8 %all-to-all-start = ((bf16[4,64,8,128]{3,2,1,0:T(8,128)(2,1)}), bf16[4,64,8,128]{3,2,1,0:T(8,128)(2,1)S(1)}, u32[]{:S(2)}, u32[]{:S(2)}) async-start(bf16[4,64,8,128]{3,2,1,0:T(8,128)(2,1)} %shard_map.91), calls=%async_computation | async-start | bytes 1048576 | tf_op jit(solution)/shard_map/all_to_all | solution.py:464
  16.1 14.6 %collective-permute-start = (bf16[256,8,128]{2,1,0:T(8,128)(2,1)S(1)}, bf16[256,8,128]{2,1,0:T(8,128)(2,1)S(1)}, u32[]{:S(2)}, u32[]{:S(2)}) collective-permute-start(bf16[256,8,128]{2,1,0:T(8,128)(2,1)S(1)} %bitcast.4), channel_id=1, source_target_pairs={{0,1},{1,0},{2,3},{3,2},{4,5},{5,4},{6,7},{7,6},{8,9},{9,8},{10,11... | collective-permute-start | bytes 1572872 | tf_op jit(solution)/shard_map/ppermute | solution.py:471
